TPU v7x, 256 devices: a whole 4x4x8 slice. The times are simulated.
256 devices in a mesh: dp: 8 (over x_lo, y), seq: 32 (over x_hi, z, core).
Axes of the slice: x: 4 (x_hi: 2, x_lo: 2; x = x_hi * 2 + x_lo), y: 4, z: 8, core: 2. Of those that a mesh axis runs over, the one named last changes fastest.
Arguments:
- queries: bfloat16 [32768, 2048], P(('dp', 'seq')), may hold values from -12 to 12
- key_rows: bfloat16 [32768, 2048], P(('dp', 'seq')), may hold values from -12 to 12
- value_rows: bfloat16 [32768, 2048], P(('dp', 'seq')), may hold values from -6 to 6
- document_ids: int32 [8, 4096], P('dp'), may hold values from 0 to 31, never falling along the last dimension, each value on 1 to 512 neighbouring positions
- link_lists: int32 [8, 32, 8], P('dp'), may hold values from 0 to 31, as said below
- block_keep: int32 [8, 32, 32], P('dp'), may hold values 0 or 1
- out_gain: float32 [2048], replicated, may hold values from 0.1 to 1.9
- cotangent: bfloat16 [32768, 2048], P(('dp', 'seq')), may hold values from -0.25 to 0.25
Outputs:
- attended: bfloat16 [32768, 2048], P(('dp', 'seq'))
- gain_grad: float32 [2048], P(('dp', 'seq'))
Inputs may be any that keep to these rules, and one draw needn't show every extreme that they name: `link_lists`: each target document lies within 3 documents of its source.
All inputs are finite; a program needn't handle non-finite values. No bound on the sum of `block_keep` on one device may be relied on, other than what follows from the above.
Results may differ from a plain program's by a relative error of at most 0.0035.
Values may be sent and summed in bfloat16 or wider, within the bound.
No kernel may reach another device: no remote copies, remote signals or barrier semaphores. Data moves between devices by JAX's collectives and lax.ppermute only.
A program may use at most 64 MiB of HBM per device.

v0:
```python
import functools
import math

import jax
import jax.numpy as jnp
from jax import lax
from jax.experimental import pallas as pl
from jax.experimental.pallas import tpu as pltpu
from jax.sharding import PartitionSpec as P

HEADS = 32
HDIM = 64
REACH = 3
BLK = 128
HALF = HEADS * HDIM // 2
PAIRS = HALF // 128
NEGATIVE_FILL = -1e30
AXES = ("dp", "seq")


def split_kernel(key_ref, value_ref, query_ref, cotangent_ref, own_ref, send_ref, send_qc_ref, sems):
    core = lax.axis_index("seq") % 2
    mine = pl.ds(pl.multiple_of(core * HALF, HALF), HALF)
    others = pl.ds(pl.multiple_of((1 - core) * HALF, HALF), HALF)
    moves = [(key_ref, mine, own_ref, 0), (value_ref, mine, own_ref, 1)]
    moves += [(key_ref, others, send_ref, 0), (value_ref, others, send_ref, 1)]
    moves += [(query_ref, others, send_qc_ref, 0), (cotangent_ref, others, send_qc_ref, 1)]
    copies = []
    for at, (source, columns, target, part) in enumerate(moves):
        copies.append(pltpu.make_async_copy(source.at[:, columns], target.at[cols(part)], sems.at[at]))
    for copy in copies:
        copy.start()
    for copy in copies:
        copy.wait()


def split_heads(*arrays):
    shape = pltpu.VMEM((2 * BLK, HALF), jnp.bfloat16)
    return pl.pallas_call(
        split_kernel,
        in_specs=[pl.BlockSpec(memory_space=pl.ANY)] * 4,
        out_specs=[pl.BlockSpec(memory_space=pltpu.VMEM)] * 3,
        out_shape=[shape] * 3,
        scratch_shapes=[pltpu.SemaphoreType.DMA((6,))],
        cost_estimate=pl.CostEstimate(flops=0, bytes_accessed=3 << 20, transcendentals=0),
    )(*arrays)


OWN, SIB, R1, R2, R3, R4, R5, R6 = range(8)
TILES = (
    [(q, k) for q in (OWN, SIB) for k in (OWN, SIB)]
    + [(q, k) for q in (OWN, SIB) for k in (R1, R2)]
    + [(q, k) for q in (OWN, SIB) for k in (R3, R4)]
    + [(SIB, R5), (OWN, R6)]
)


def key_blocks():
    place = lax.axis_index("seq")
    chip, core = place // 2, place % 2
    toward = 1 - 2 * core
    ring = [(chip, core), (chip, 1 - core)]
    ring += [(chip + toward, core), (chip - toward, 1 - core), (chip - toward, core), (chip + toward, 1 - core)]
    ring += [(chip + 2 * toward, core), (chip - 2 * toward, 1 - core)]
    return [2 * at + side for at, side in ring]


def mask_kernel(keep_ref, docs_ref, links_ref, bias_ref):
    docs_in_pack = links_ref.shape[1]
    nblk = docs_ref.shape[1] // BLK
    blocks = key_blocks()
    target = lax.broadcasted_iota(jnp.int32, (docs_in_pack, docs_in_pack), 1)
    source = lax.broadcasted_iota(jnp.int32, (docs_in_pack, docs_in_pack), 0)
    links = links_ref[0]
    linked = target == links[:, 0:1]
    for at in range(1, links.shape[1]):
        linked = linked | (target == links[:, at : at + 1])
    table = jnp.where(source == target, 2.0, 0.0) + jnp.where(linked, 1.0, 0.0)
    table = table.astype(jnp.bfloat16)

    def one_hot(block):
        at = pl.multiple_of(jnp.clip(block, 0, nblk - 1) * BLK, BLK)
        row = docs_ref[:, pl.ds(at, BLK)]
        rows = lax.broadcasted_iota(jnp.int32, (docs_in_pack, BLK), 0)
        return jnp.where(rows == row, 1.0, 0.0).astype(jnp.bfloat16)

    hots = [one_hot(block) for block in blocks]
    related = [
        lax.dot_general(table, hots[q], (((0,), (0,)), ((), ())), preferred_element_type=jnp.float32).astype(jnp.bfloat16)
        for q in (OWN, SIB)
    ]
    key_at = lax.broadcasted_iota(jnp.int32, (BLK, BLK), 0)
    query_at = lax.broadcasted_iota(jnp.int32, (BLK, BLK), 1)
    apart = query_at - key_at
    for tile, (q, k) in enumerate(TILES):
        query_block, key_block = blocks[q], blocks[k]
        present = (key_block >= 0) & (key_block < nblk)
        kept = keep_ref[0, query_block, jnp.clip(key_block, 0, nblk - 1)] == 1
        least = jnp.where(present, jnp.where(kept, 0.5, 1.5), 9.0)
        relation = lax.dot_general(hots[k], related[q], (((0,), (0,)), ((), ())), preferred_element_type=jnp.float32)
        distance = apart + (query_block - key_block) * BLK
        allowed = (relation > least) & (jnp.abs(distance) <= REACH * BLK)
        bias_ref[tile * BLK : (tile + 1) * BLK] = jnp.where(allowed, 0.0, NEGATIVE_FILL)


def masks(keep, docs, links):
    return in_vmem(mask_kernel, 1, [pltpu.VMEM((len(TILES) * BLK, BLK), jnp.float32)], keep, docs, links, scalars=1)[0]


def absorb(queries, keys, values, biases, state):
    stacked = []
    for query in queries:
        low = lax.broadcasted_iota(jnp.int32, query.shape, 1) < HDIM
        scaled = query * jnp.bfloat16(1.0 / math.sqrt(HDIM))
        nothing = jnp.zeros_like(scaled)
        stacked += [jnp.where(low, scaled, nothing), jnp.where(low, nothing, scaled)]
    scores = lax.dot_general(
        keys, jnp.concatenate(stacked, axis=0), (((1,), (1,)), ((), ())), preferred_element_type=jnp.float32
    )
    scores = scores + jnp.concatenate([bias for bias in biases for _ in range(2)], axis=1)
    largest = jnp.max(scores, axis=0, keepdims=True)
    if state is not None:
        largest = jnp.maximum(state[0], largest)
    expo = jnp.exp(scores - largest)
    totals = jnp.sum(expo, axis=0, keepdims=True)
    sums = lax.dot_general(
        values, expo.astype(jnp.bfloat16), (((0,), (0,)), ((), ())), preferred_element_type=jnp.float32
    )
    folded = fold(sums[:HDIM], sums[HDIM:])
    if state is not None:
        shrink = jnp.exp(state[0] - largest)
        totals = totals + state[1] * shrink
        folded = folded + state[2] * spread(shrink)
    return largest, totals, folded


def fold(first, second):
    blocks = range(0, first.shape[1], 2 * BLK)
    pieces = [jnp.concatenate([first[:, at : at + BLK], second[:, at + BLK : at + 2 * BLK]], axis=0) for at in blocks]
    return jnp.concatenate(pieces, axis=1)


def spread(row):
    wide = jnp.broadcast_to(row, (HDIM, row.shape[1]))
    return fold(wide, wide)


def cols(at):
    return slice(at * BLK, (at + 1) * BLK)


def my_cols(at):
    core = lax.axis_index("seq") % 2
    return pl.ds(pl.multiple_of(core * HALF + at * BLK, BLK), BLK)


def put_state(rows_ref, sums_ref, at, state):
    rows_ref[at * 8 : at * 8 + 1] = state[0]
    rows_ref[at * 8 + 1 : at * 8 + 2] = state[1]
    sums_ref[cols(at)] = state[2]


def get_state(rows_ref, sums_ref, at, first=0, blocks=2):
    of_rows = slice(first * 2 * BLK, (first + blocks) * 2 * BLK)
    of_sums = slice(first * BLK, (first + blocks) * BLK)
    return rows_ref[at * 8 : at * 8 + 1, of_rows], rows_ref[at * 8 + 1 : at * 8 + 2, of_rows], sums_ref[cols(at), of_sums]


def both_kernel(tile, bias_ref, query_ref, qc_sib, kv_a, kv_b, *states):
    before, now = states[:-2], states[-2:]
    for at in range(PAIRS):
        at_cols = cols(at)
        keys = jnp.concatenate([kv_a[:BLK, at_cols], kv_b[:BLK, at_cols]], axis=0)
        values = jnp.concatenate([kv_a[BLK:, at_cols], kv_b[BLK:, at_cols]], axis=0)
        queries = [query_ref[:, my_cols(at)], qc_sib[:BLK, at_cols]]
        biases = [bias_ref[(tile + 2 * side) * BLK : (tile + 2 * side + 2) * BLK] for side in range(2)]
        state = get_state(*before, at) if before else None
        put_state(*now, at, absorb(queries, keys, values, biases, state))


def finish(state, gain, cotangent):
    mixed = jnp.transpose(state[2] / spread(state[1]))
    attended = (gain * mixed).astype(jnp.bfloat16)
    terms = jnp.sum(mixed * cotangent.astype(jnp.float32), axis=0, keepdims=True)
    return attended, terms


def last(tile, side, at, bias_ref, query, cotangent, kv, rows, sums, gain_ref):
    at_cols = cols(at)
    state = get_state(rows, sums, at, side, 1)
    state = absorb([query], kv[:BLK, at_cols], kv[BLK:, at_cols], [bias_ref[cols(tile)]], state)
    return finish(state, gain_ref[:, my_cols(at)], cotangent)


def sib_kernel(bias_ref, qc, kv, rows, sums, gain_ref, att_ref, terms_ref):
    for at in range(PAIRS):
        query, cotangent = qc[:BLK, cols(at)], qc[BLK:, cols(at)]
        att_ref[:, cols(at)], terms = last(12, 1, at, bias_ref, query, cotangent, kv, rows, sums, gain_ref)
        terms_ref[at : at + 1] = terms


def own_kernel(
    bias_ref, query_ref, cotangent_ref, kv, rows, sums, gain_ref, terms_in, out_ref, terms_ref, att, spread_terms, sems
):
    core = lax.axis_index("seq") % 2
    devices = terms_ref.shape[0] // (2 * PAIRS)
    copies = []

    def send(source, target):
        copies.append(pltpu.make_async_copy(source, target, sems.at[len(copies)]))
        copies[-1].start()

    half = PAIRS * devices
    here = pl.ds(pl.multiple_of((1 - core) * half, half), half)
    spread_terms[here] = jnp.zeros((half, BLK), jnp.float32)
    send(spread_terms.at[here], terms_ref.at[here])
    for at in range(PAIRS):
        query, cotangent = query_ref[:, my_cols(at)], cotangent_ref[:, my_cols(at)]
        att[:, cols(at)], terms = last(13, 0, at, bias_ref, query, cotangent, kv, rows, sums, gain_ref)
        send(att.at[:, cols(at)], out_ref.at[:, my_cols(at)])
        here = pl.ds(pl.multiple_of((core * PAIRS + at) * devices, devices), devices)
        spread_terms[here] = jnp.broadcast_to(terms + terms_in[at : at + 1], (devices, BLK))
        send(spread_terms.at[here], terms_ref.at[here])
    for copy in copies:
        copy.wait()


def fill_kernel(back_ref, out_in, out_ref, sem):
    core = lax.axis_index("seq") % 2
    there = pl.ds(pl.multiple_of((1 - core) * HALF, HALF), HALF)
    copy = pltpu.make_async_copy(back_ref, out_ref.at[:, there], sem)
    copy.start()
    copy.wait()


def fill_heads(back, out):
    return pl.pallas_call(
        fill_kernel,
        in_specs=[pl.BlockSpec(memory_space=pltpu.VMEM), pl.BlockSpec(memory_space=pl.ANY)],
        out_specs=pl.BlockSpec(memory_space=pl.ANY),
        out_shape=jax.ShapeDtypeStruct(out.shape, out.dtype),
        input_output_aliases={1: 0},
        scratch_shapes=[pltpu.SemaphoreType.DMA],
        cost_estimate=pl.CostEstimate(flops=0, bytes_accessed=1 << 20, transcendentals=0),
    )(back, out)


STATE = [pltpu.VMEM((PAIRS * 8, 4 * BLK), jnp.float32), pltpu.VMEM((PAIRS * BLK, 2 * BLK), jnp.float32)]


def in_vmem(kernel, tiles, outputs, *operands, scalars=0):
    vmem = pl.BlockSpec(memory_space=pltpu.VMEM)
    smem = pl.BlockSpec(memory_space=pltpu.SMEM)
    cost = pl.CostEstimate(
        flops=tiles * 64 * BLK * BLK * HDIM, bytes_accessed=1 << 20, transcendentals=tiles * 16 * BLK * BLK
    )
    return pl.pallas_call(
        kernel,
        in_specs=[smem] * scalars + [vmem] * (len(operands) - scalars),
        out_specs=[vmem] * len(outputs),
        out_shape=outputs,
        cost_estimate=cost,
        compiler_params=pltpu.CompilerParams(vmem_limit_bytes=8 << 20),
    )(*operands)


def both(tile, bias, queries, qc_sib, kv_a, kv_b, state=()):
    return in_vmem(functools.partial(both_kernel, tile), 4, STATE, bias, queries, qc_sib, kv_a, kv_b, *state)


def last_sib(*operands):
    outputs = [pltpu.VMEM((BLK, HALF), jnp.bfloat16), pltpu.VMEM((PAIRS, BLK), jnp.float32)]
    return in_vmem(sib_kernel, 1, outputs, *operands)


def last_own(devices, *operands):
    return pl.pallas_call(
        own_kernel,
        in_specs=[pl.BlockSpec(memory_space=pltpu.VMEM)] * len(operands),
        out_specs=[pl.BlockSpec(memory_space=pl.ANY)] * 2,
        out_shape=[
            jax.ShapeDtypeStruct((BLK, 2 * HALF), jnp.bfloat16),
            jax.ShapeDtypeStruct((devices, BLK), jnp.float32),
        ],
        scratch_shapes=[
            pltpu.VMEM((BLK, HALF), jnp.bfloat16),
            pltpu.VMEM((devices, BLK), jnp.float32),
            pltpu.SemaphoreType.DMA((1 + 2 * PAIRS,)),
        ],
        cost_estimate=pl.CostEstimate(flops=64 * BLK * BLK * HDIM, bytes_accessed=1 << 20, transcendentals=16 * BLK * BLK),
        compiler_params=pltpu.CompilerParams(vmem_limit_bytes=8 << 20),
    )(*operands)


def sum_kernel(pieces_ref, out_ref):
    mine = out_ref.shape[1]
    place = lax.axis_index("dp") * lax.axis_size("seq") + lax.axis_index("seq")
    total = jnp.sum(pieces_ref[...], axis=0, keepdims=True)
    at = lax.rem(place, BLK // mine) * mine
    out_ref[...] = pltpu.roll(total, lax.rem(BLK - at, BLK), 1)[:, :mine]


def rotations(groups, shards):
    onward = []
    for group in range(groups):
        for place in range(shards):
            chip, core = divmod(place, 2)
            there = chip + (1 if core == 1 else -1)
            target = there * 2 + core if 0 <= there < shards // 2 else chip * 2 + 1 - core
            onward.append((group * shards + place, group * shards + target))
    backward = [(target, source) for source, target in onward]
    crossing = lambda ring: [(at, to ^ 1 if to // 2 != at // 2 else at) for at, to in ring]
    return onward, backward, crossing(onward), crossing(backward)


def after(value, *others):
    return lax.optimization_barrier((value, *others))[0]


def local(queries, key_rows, value_rows, document_ids, link_lists, block_keep, out_gain, cotangent):
    groups, shards = lax.axis_size("dp"), lax.axis_size("seq")
    onward, backward, outward, inward = rotations(groups, shards)
    siblings = [(i, i ^ 1) for i in range(groups * shards)]
    move = lambda value, pairs: lax.ppermute(value, AXES, pairs)
    gain = out_gain.reshape(1, -1)

    kv_own, kv_send, qc_send = split_heads(key_rows, value_rows, queries, cotangent)
    r1 = move(kv_own, onward)
    r2 = move(kv_send, outward)
    kv_sib = move(kv_send, siblings)
    qc_sib = move(qc_send, siblings)
    bias = masks(block_keep, document_ids, link_lists)
    r3 = move(after(kv_own, qc_sib), backward)
    r4 = move(after(kv_send, qc_sib), inward)
    r5 = move(r1, onward)
    state = both(0, bias, queries, qc_sib, kv_own, kv_sib)
    r6 = move(after(r2, *state), backward)
    state = both(4, bias, queries, qc_sib, r1, r2, state)
    state = both(8, bias, queries, qc_sib, r3, r4, state)
    att_sib, terms = last_sib(bias, qc_sib, r5, *state, gain)
    back = move(att_sib, siblings)
    out, terms = last_own(groups * shards, bias, queries, cotangent, r6, *state, gain, terms)
    pieces = lax.all_to_all(terms.reshape(groups * shards, 1, BLK), AXES, 0, 0, tiled=True)
    attended = fill_heads(back, out)
    pieces = after(pieces, attended)
    mine = jax.ShapeDtypeStruct((1, 2 * HALF // (groups * shards)), jnp.float32)
    (gain_grad,) = in_vmem(sum_kernel, 0, [mine], pieces.reshape(groups * shards, BLK))
    return attended, gain_grad.reshape(-1)


def solution(mesh):
    placed = (
        P(AXES, None),
        P(AXES, None),
        P(AXES, None),
        P("dp", None),
        P("dp", None, None),
        P("dp", None, None),
        P(),
        P(AXES, None),
    )
    return jax.shard_map(local, mesh=mesh, in_specs=placed, out_specs=(P(AXES, None), P(AXES)), check_vma=False)
```

profile of v0, /device:TPU:1, one launch (start us, length us, event | category | flops | bytes accessed | tf_op | source)
XLA Modules:
  0.0 72.0 jit_solution(10295199021817439884)
XLA Ops:
  0.7 2.4 %shard_map.96 = (bf16[256,1024]{1,0:T(8,128)(2,1)S(1)}, bf16[256,1024]{1,0:T(8,128)(2,1)}, bf16[256,1024]{1,0:T(8,128)(2,1)}) custom-call(bf16[128,2048]{1,0:T(8,128)(2,1)} %key_ref.1, bf16[128,2048]{1,0:T(8,128)(2,1)} %value_ref.1, bf16[128,2048]{1,0:T(8,128)(2,1)} %query_ref.9, bf16[128,2048]{1,0:T(8,128)(2,1)} %cotangent_ref.3), custom_call_target="tpu_custom_call" | custom-call | bytes 3145728 | tf_op jit(solution)/shard_map/pallas_call | solution.py:39
  3.1 3.3 %collective-permute-start = (bf16[256,1024]{1,0:T(8,128)(2,1)}, bf16[256,1024]{1,0:T(8,128)(2,1)S(1)}, u32[]{:S(2)}, u32[]{:S(2)}) collective-permute-start(bf16[256,1024]{1,0:T(8,128)(2,1)} %get-tuple-element.19), channel_id=1, source_target_pairs={{0,1},{1,0},{2,3},{3,2},{4,5},{5,4},{6,7},{7,6},{8,9},{9,8},{10,11... | collective-permute-start | bytes 1572872 | tf_op jit(solution)/shard_map/ppermute | solution.py:324
  6.4 0.5 collective-permute-start.6
  6.9 3.3 %collective-permute-start.5 = (bf16[256,1024]{1,0:T(8,128)(2,1)}, bf16[256,1024]{1,0:T(8,128)(2,1)S(1)}, u32[]{:S(2)}, u32[]{:S(2)}) collective-permute-start(bf16[256,1024]{1,0:T(8,128)(2,1)} %get-tuple-element.23), channel_id=1, source_target_pairs={{0,0},{1,2},{2,1},{3,4},{4,3},{5,6},{6,5},{7,8},{8,7},{9,10},{10,9... | collective-permute-start | bytes 1572872 | tf_op jit(solution)/shard_map/ppermute | solution.py:324
  10.2 0.1 copy.12.links_ref
  10.3 0.0 collective-permute-start.3
  10.4 1.7 %collective-permute-start.4 = (bf16[256,1024]{1,0:T(8,128)(2,1)}, bf16[256,1024]{1,0:T(8,128)(2,1)S(1)}, u32[]{:S(2)}, u32[]{:S(2)}) collective-permute-start(bf16[256,1024]{1,0:T(8,128)(2,1)} %get-tuple-element.23), channel_id=1, source_target_pairs={{1,1},{3,0},{0,3},{5,2},{2,5},{7,4},{4,7},{9,6},{6,9},{11,8},{8,11... | collective-permute-start | bytes 1572872 | tf_op jit(solution)/shard_map/ppermute | solution.py:324
  12.1 1.4 %shard_map.95.bias_ref = f32[1792,128]{1,0:T(8,128)S(1)} custom-call(s32[1,32,32]{2,1,0:T(8,128)S(1)} %copy-done.3, s32[1,4096]{1,0:T(1,128)S(1)} %copy-done.4, s32[1,32,8]{2,1,0:T(8,128)S(1)} %copy.12.links_ref), custom_call_target="tpu_custom_call" | custom-call | flops 67108864 | bytes 1048576 | tf_op jit(solution)/shard_map/pallas_call | solution.py:257
  13.4 2.3 %collective-permute-start.2 = (bf16[256,1024]{1,0:T(8,128)(2,1)}, bf16[256,1024]{1,0:T(8,128)(2,1)S(1)}, u32[]{:S(2)}, u32[]{:S(2)}) collective-permute-start(bf16[256,1024]{1,0:T(8,128)(2,1)} %collective-permute-done.1.kv_a), channel_id=1, source_target_pairs={{0,1},{1,3},{2,0},{3,5},{4,2},{5,7},{6,4},{7,9},{8,6},{9,11},{10,8... | collective-permute-start | bytes 1572872 | tf_op jit(solution)/shard_map/ppermute | solution.py:324
  15.8 2.9 %shard_map.97 = (f32[64,512]{1,0:T(8,128)S(1)}, f32[1024,256]{1,0:T(8,128)S(1)}) custom-call(f32[1792,128]{1,0:T(8,128)S(1)} %shard_map.95.bias_ref, bf16[128,2048]{1,0:T(8,128)(2,1)S(1)} %copy-done, bf16[256,1024]{1,0:T(8,128)(2,1)S(1)} %collective-permute-done.qc_sib.qc, bf16[256,1024]{1,0:T(8,128)(2,1)S(1)} %get-tuple-element.21.kv_a, ...), custom_call_target="tpu_custom_call" | custom-call | flops 268435456 | bytes 1048576 | tf_op jit(solution)/shard_map/pallas_call | solution.py:257
  18.7 9.8 %collective-permute-done.5.kv_b = bf16[256,1024]{1,0:T(8,128)(2,1)S(1)} collective-permute-done((bf16[256,1024]{1,0:T(8,128)(2,1)}, bf16[256,1024]{1,0:T(8,128)(2,1)S(1)}, u32[]{:S(2)}, u32[]{:S(2)}) %collective-permute-start.5) | collective-permute-done | bytes 524320 | tf_op jit(solution)/shard_map/ppermute | solution.py:324
  28.5 4.0 %shard_map.98 = (f32[64,512]{1,0:T(8,128)S(1)}, f32[1024,256]{1,0:T(8,128)S(1)}) custom-call(f32[1792,128]{1,0:T(8,128)S(1)} %shard_map.95.bias_ref, bf16[128,2048]{1,0:T(8,128)(2,1)S(1)} %copy-done, bf16[256,1024]{1,0:T(8,128)(2,1)S(1)} %collective-permute-done.qc_sib.qc, bf16[256,1024]{1,0:T(8,128)(2,1)} %collective-permute-done.1.kv_a, ...), custom_call_target="tpu_custom_call" | custom-call | flops 268435456 | bytes 1048576 | tf_op jit(solution)/shard_map/pallas_call | solution.py:257
  32.6 0.0 copy-start.2
  32.6 3.0 %shard_map.99 = (f32[64,512]{1,0:T(8,128)S(1)}, f32[1024,256]{1,0:T(8,128)S(1)}) custom-call(f32[1792,128]{1,0:T(8,128)S(1)} %shard_map.95.bias_ref, bf16[128,2048]{1,0:T(8,128)(2,1)S(1)} %copy-done, bf16[256,1024]{1,0:T(8,128)(2,1)S(1)} %collective-permute-done.qc_sib.qc, bf16[256,1024]{1,0:T(8,128)(2,1)S(1)} %collective-permute-done.3.kv_a, ...), custom_call_target="tpu_custom_call" | custom-call | flops 268435456 | bytes 1048576 | tf_op jit(solution)/shard_map/pallas_call | solution.py:257
  35.6 0.2 collective-permute-done.2.kv
  35.8 0.9 %shard_map.100 = (bf16[128,1024]{1,0:T(8,128)(2,1)S(1)}, f32[8,128]{1,0:T(8,128)S(1)}) custom-call(f32[1792,128]{1,0:T(8,128)S(1)} %shard_map.95.bias_ref, bf16[256,1024]{1,0:T(8,128)(2,1)S(1)} %collective-permute-done.qc_sib.qc, bf16[256,1024]{1,0:T(8,128)(2,1)S(1)} %collective-permute-done.2.kv, f32[64,512]{1,0:T(8,128)S(1)} %get-tuple-element.28.rows, ...), custom_call_target="tpu_custom_call" | custom-call | flops 67108864 | bytes 1048576 | tf_op jit(solution)/shard_map/pallas_call | solution.py:257
  36.7 4.4 %collective-permute-start.7 = (bf16[128,1024]{1,0:T(8,128)(2,1)S(1)}, bf16[128,1024]{1,0:T(8,128)(2,1)S(1)}, u32[]{:S(2)}, u32[]{:S(2)}) collective-permute-start(bf16[128,1024]{1,0:T(8,128)(2,1)S(1)} %get-tuple-element.30), channel_id=1, source_target_pairs={{0,1},{1,0},{2,3},{3,2},{4,5},{5,4},{6,7},{7,6},{8,9},{9,8},{10,11... | collective-permute-start | bytes 786440 | tf_op jit(solution)/shard_map/ppermute | solution.py:324
  41.1 1.9 %collective-permute-done.8.kv = bf16[256,1024]{1,0:T(8,128)(2,1)S(1)} collective-permute-done((bf16[256,1024]{1,0:T(8,128)(2,1)S(1)}, bf16[256,1024]{1,0:T(8,128)(2,1)S(1)}, u32[]{:S(2)}, u32[]{:S(2)}) %collective-permute-start.8) | collective-permute-done | bytes 524320 | tf_op jit(solution)/shard_map/ppermute | solution.py:324
  43.1 1.7 %shard_map.101 = (bf16[128,2048]{1,0:T(8,128)(2,1)}, f32[256,128]{1,0:T(8,128)}) custom-call(f32[1792,128]{1,0:T(8,128)S(1)} %shard_map.95.bias_ref, bf16[128,2048]{1,0:T(8,128)(2,1)S(1)} %copy-done, bf16[128,2048]{1,0:T(8,128)(2,1)S(1)} %copy-done.1, bf16[256,1024]{1,0:T(8,128)(2,1)S(1)} %collective-permute-done.8.kv, ...), custom_call_target="tpu_custom_call" | custom-call | flops 67108864 | bytes 1048576 | tf_op jit(solution)/shard_map/pallas_call | solution.py:277
  44.8 13.8 %all-to-all-start = ((f32[256,1,128]{2,1,0:T(1,128)}), f32[256,1,128]{2,1,0:T(1,128)S(1)}, u32[]{:S(2)}, u32[]{:S(2)}) async-start(f32[256,1,128]{2,1,0:T(1,128)} %bitcast.2), calls=%async_computation | async-start | bytes 262144 | tf_op jit(solution)/shard_map/all_to_all | solution.py:343
  58.6 0.7 copy-done.5
  59.3 1.7 %shard_map.102 = bf16[128,2048]{1,0:T(8,128)(2,1)} custom-call(bf16[128,1024]{1,0:T(8,128)(2,1)} %copy-done.5, bf16[128,2048]{1,0:T(8,128)(2,1)} %get-tuple-element.33.out_in), custom_call_target="tpu_custom_call", output_to_operand_aliasing={{}: (1, {})} | custom-call | bytes 1048576 | tf_op jit(solution)/shard_map/pallas_call | solution.py:237
  60.9 10.4 %all-to-all-done = f32[256,1,128]{2,1,0:T(1,128)S(1)} async-done(((f32[256,1,128]{2,1,0:T(1,128)}), f32[256,1,128]{2,1,0:T(1,128)S(1)}, u32[]{:S(2)}, u32[]{:S(2)}) %all-to-all-start) | async-done | bytes 131104 | tf_op jit(solution)/shard_map/all_to_all | solution.py:343
  71.4 0.6 shard_map.103
  (20 shorter events, 0.0 us)
Async XLA Ops:
  0.6 9.6 %copy-start.6 = (s32[1,32,8]{1,2,0:T(8,128)S(1)}, s32[1,32,8]{1,2,0:T(8,128)}, u32[]{:S(2)}) copy-start(s32[1,32,8]{1,2,0:T(8,128)} %param.12) | copy-start | bytes 3076
  0.6 11.4 %copy-start.3 = (s32[1,32,32]{2,1,0:T(8,128)S(1)}, s32[1,32,32]{2,1,0:T(8,128)}, u32[]{:S(2)}) copy-start(s32[1,32,32]{2,1,0:T(8,128)} %keep_ref.1) | copy-start | bytes 12292
  0.7 11.4 %copy-start.4 = (s32[1,4096]{1,0:T(1,128)S(1)}, s32[1,4096]{1,0:T(1,128)}, u32[]{:S(2)}) copy-start(s32[1,4096]{1,0:T(1,128)} %docs_ref.1) | copy-start | bytes 49156
  3.1 12.7 %copy-start = (bf16[128,2048]{1,0:T(8,128)(2,1)S(1)}, bf16[128,2048]{1,0:T(8,128)(2,1)}, u32[]{:S(2)}) copy-start(bf16[128,2048]{1,0:T(8,128)(2,1)} %query_ref.9) | copy-start | bytes 1572868
  3.1 7.3 %collective-permute-start = (bf16[256,1024]{1,0:T(8,128)(2,1)}, bf16[256,1024]{1,0:T(8,128)(2,1)S(1)}, u32[]{:S(2)}, u32[]{:S(2)}) collective-permute-start(bf16[256,1024]{1,0:T(8,128)(2,1)} %get-tuple-element.19), channel_id=1, source_target_pairs={{0,1},{1,0},{2,3},{3,2},{4,5},{5,4},{6,7},{7,6},{8,9},{9,8},{10,11... | collective-permute-start | bytes 1572872 | tf_op jit(solution)/shard_map/ppermute | solution.py:324
  6.4 7.0 %collective-permute-start.1 = (bf16[256,1024]{1,0:T(8,128)(2,1)S(1)}, bf16[256,1024]{1,0:T(8,128)(2,1)}, u32[]{:S(2)}, u32[]{:S(2)}) collective-permute-start(bf16[256,1024]{1,0:T(8,128)(2,1)S(1)} %get-tuple-element.21.kv_a), channel_id=1, source_target_pairs={{0,1},{1,3},{2,0},{3,5},{4,2},{5,7},{6,4},{7,9},{8,6},{9,11},{10,8... | collective-permute-start | bytes 1572872 | tf_op jit(solution)/shard_map/ppermute | solution.py:324
  6.4 9.4 %collective-permute-start.6 = (bf16[256,1024]{1,0:T(8,128)(2,1)}, bf16[256,1024]{1,0:T(8,128)(2,1)S(1)}, u32[]{:S(2)}, u32[]{:S(2)}) collective-permute-start(bf16[256,1024]{1,0:T(8,128)(2,1)} %get-tuple-element.23), channel_id=1, source_target_pairs={{0,1},{1,0},{2,3},{3,2},{4,5},{5,4},{6,7},{7,6},{8,9},{9,8},{10,11... | collective-permute-start | bytes 1572872 | tf_op jit(solution)/shard_map/ppermute | solution.py:324
  6.9 21.6 %collective-permute-start.5 = (bf16[256,1024]{1,0:T(8,128)(2,1)}, bf16[256,1024]{1,0:T(8,128)(2,1)S(1)}, u32[]{:S(2)}, u32[]{:S(2)}) collective-permute-start(bf16[256,1024]{1,0:T(8,128)(2,1)} %get-tuple-element.23), channel_id=1, source_target_pairs={{0,0},{1,2},{2,1},{3,4},{4,3},{5,6},{6,5},{7,8},{8,7},{9,10},{10,9... | collective-permute-start | bytes 1572872 | tf_op jit(solution)/shard_map/ppermute | solution.py:324
  10.3 22.2 %collective-permute-start.3 = (bf16[256,1024]{1,0:T(8,128)(2,1)S(1)}, bf16[256,1024]{1,0:T(8,128)(2,1)S(1)}, u32[]{:S(2)}, u32[]{:S(2)}) collective-permute-start(bf16[256,1024]{1,0:T(8,128)(2,1)S(1)} %get-tuple-element.21.kv_a), channel_id=1, source_target_pairs={{1,0},{3,1},{0,2},{5,3},{2,4},{7,5},{4,6},{9,7},{6,8},{11,9},{8,10... | collective-permute-start | bytes 1572872 | tf_op jit(solution)/shard_map/ppermute | solution.py:324
  10.4 22.2 %collective-permute-start.4 = (bf16[256,1024]{1,0:T(8,128)(2,1)}, bf16[256,1024]{1,0:T(8,128)(2,1)S(1)}, u32[]{:S(2)}, u32[]{:S(2)}) collective-permute-start(bf16[256,1024]{1,0:T(8,128)(2,1)} %get-tuple-element.23), channel_id=1, source_target_pairs={{1,1},{3,0},{0,3},{5,2},{2,5},{7,4},{4,7},{9,6},{6,9},{11,8},{8,11... | collective-permute-start | bytes 1572872 | tf_op jit(solution)/shard_map/ppermute | solution.py:324
  13.4 22.4 %collective-permute-start.2 = (bf16[256,1024]{1,0:T(8,128)(2,1)}, bf16[256,1024]{1,0:T(8,128)(2,1)S(1)}, u32[]{:S(2)}, u32[]{:S(2)}) collective-permute-start(bf16[256,1024]{1,0:T(8,128)(2,1)} %collective-permute-done.1.kv_a), channel_id=1, source_target_pairs={{0,1},{1,3},{2,0},{3,5},{4,2},{5,7},{6,4},{7,9},{8,6},{9,11},{10,8... | collective-permute-start | bytes 1572872 | tf_op jit(solution)/shard_map/ppermute | solution.py:324
  28.5 14.6 %collective-permute-start.8 = (bf16[256,1024]{1,0:T(8,128)(2,1)S(1)}, bf16[256,1024]{1,0:T(8,128)(2,1)S(1)}, u32[]{:S(2)}, u32[]{:S(2)}) collective-permute-start(bf16[256,1024]{1,0:T(8,128)(2,1)S(1)} %collective-permute-done.5.kv_b), channel_id=1, source_target_pairs={{1,0},{3,1},{0,2},{5,3},{2,4},{7,5},{4,6},{9,7},{6,8},{11,9},{8,10... | collective-permute-start | bytes 1572872 | tf_op jit(solution)/shard_map/ppermute | solution.py:324
  32.6 3.2 %copy-start.2 = (f32[2048]{0:T(1024)S(1)}, f32[2048]{0:T(1024)}, u32[]{:S(2)}) copy-start(f32[2048]{0:T(1024)} %param.14) | copy-start | bytes 24580
  35.8 7.3 %copy-start.1 = (bf16[128,2048]{1,0:T(8,128)(2,1)S(1)}, bf16[128,2048]{1,0:T(8,128)(2,1)}, u32[]{:S(2)}) copy-start(bf16[128,2048]{1,0:T(8,128)(2,1)} %cotangent_ref.3) | copy-start | bytes 1572868
  36.7 21.8 %collective-permute-start.7 = (bf16[128,1024]{1,0:T(8,128)(2,1)S(1)}, bf16[128,1024]{1,0:T(8,128)(2,1)S(1)}, u32[]{:S(2)}, u32[]{:S(2)}) collective-permute-start(bf16[128,1024]{1,0:T(8,128)(2,1)S(1)} %get-tuple-element.30), channel_id=1, source_target_pairs={{0,1},{1,0},{2,3},{3,2},{4,5},{5,4},{6,7},{7,6},{8,9},{9,8},{10,11... | collective-permute-start | bytes 786440 | tf_op jit(solution)/shard_map/ppermute | solution.py:324
  44.8 26.6 %all-to-all-start = ((f32[256,1,128]{2,1,0:T(1,128)}), f32[256,1,128]{2,1,0:T(1,128)S(1)}, u32[]{:S(2)}, u32[]{:S(2)}) async-start(f32[256,1,128]{2,1,0:T(1,128)} %bitcast.2), calls=%async_computation | async-start | bytes 262144 | tf_op jit(solution)/shard_map/all_to_all | solution.py:343
  58.6 0.7 copy-start.5
where the time goes:
time: 72.3 us; the launch traced here: 72 us
  starting transfers between devices  29.4 us (41%)
  waiting for transfers between devices  22.4 us (31%)
  Pallas kernels  18.6 us (26%)
  between operations  0.81 us (1%)
  local copies, waits for them, and re-layouts  0.8 us (1%)
    ppermute x9, starting transfers between devices, local(): move = lambda value, pairs: lax.ppermute(value, AXES, pairs)  15.6 us
    all_to_all x1, starting transfers between devices, local(): lax.all_to_all(terms.reshape(groups * shards, 1, BLK), AXES, 0, 0, tiled=...  13.8 us
    pallas_call x6, Pallas kernels, in_vmem(): pl.pallas_call(kernel, in_specs=[smem] * scalars + [vmem] * (len(operands...  12.8 us
    ppermute x9, waiting for transfers between devices, local(): move = lambda value, pairs: lax.ppermute(value, AXES, pairs)  12 us
    all_to_all x1, waiting for transfers between devices, local(): lax.all_to_all(terms.reshape(groups * shards, 1, BLK), AXES, 0, 0, tiled=...  10.4 us
    pallas_call x1, Pallas kernels, split_heads(): pl.pallas_call(split_kernel, in_specs=[pl.BlockSpec(memory_space=pl.ANY)]...  2.39 us
    pallas_call x1, Pallas kernels, last_own(): pl.pallas_call(own_kernel, in_specs=[pl.BlockSpec(memory_space=pltpu.VMEM...  1.7 us
    pallas_call x1, Pallas kernels, fill_heads(): pl.pallas_call(fill_kernel, in_specs=[pl.BlockSpec(memory_space=pltpu.VME...  1.66 us
  transfers between devices with their start and end apart: 10, of which 4 were waited for; matrix products, arithmetic and copies ran while one was open for 0% of the time, Pallas kernels for 22%

commit v1 on v0

--- a/solution.py
+++ b/solution.py
@@ -18,31 +18,30 @@
 AXES = ("dp", "seq")
 
 
-def split_kernel(key_ref, value_ref, query_ref, cotangent_ref, own_ref, send_ref, send_qc_ref, sems):
+def split_kernel(sides, count, *refs):
+    sources, targets, sems = refs[:count], refs[count:-1], refs[-1]
     core = lax.axis_index("seq") % 2
-    mine = pl.ds(pl.multiple_of(core * HALF, HALF), HALF)
-    others = pl.ds(pl.multiple_of((1 - core) * HALF, HALF), HALF)
-    moves = [(key_ref, mine, own_ref, 0), (value_ref, mine, own_ref, 1)]
-    moves += [(key_ref, others, send_ref, 0), (value_ref, others, send_ref, 1)]
-    moves += [(query_ref, others, send_qc_ref, 0), (cotangent_ref, others, send_qc_ref, 1)]
     copies = []
-    for at, (source, columns, target, part) in enumerate(moves):
-        copies.append(pltpu.make_async_copy(source.at[:, columns], target.at[cols(part)], sems.at[at]))
+    for side, target in zip(sides, targets):
+        columns = pl.ds(pl.multiple_of((core if side == 0 else 1 - core) * HALF, HALF), HALF)
+        for part, source in enumerate(sources):
+            copy = pltpu.make_async_copy(source.at[:, columns], target.at[cols(part)], sems.at[len(copies)])
+            copies.append(copy)
     for copy in copies:
         copy.start()
     for copy in copies:
         copy.wait()
 
 
-def split_heads(*arrays):
-    shape = pltpu.VMEM((2 * BLK, HALF), jnp.bfloat16)
+def split_heads(sides, *arrays):
+    count = len(sides)
     return pl.pallas_call(
-        split_kernel,
-        in_specs=[pl.BlockSpec(memory_space=pl.ANY)] * 4,
-        out_specs=[pl.BlockSpec(memory_space=pltpu.VMEM)] * 3,
-        out_shape=[shape] * 3,
-        scratch_shapes=[pltpu.SemaphoreType.DMA((6,))],
-        cost_estimate=pl.CostEstimate(flops=0, bytes_accessed=3 << 20, transcendentals=0),
+        functools.partial(split_kernel, sides, 2),
+        in_specs=[pl.BlockSpec(memory_space=pl.ANY)] * 2,
+        out_specs=[pl.BlockSpec(memory_space=pltpu.VMEM)] * count,
+        out_shape=[pltpu.VMEM((2 * BLK, HALF), jnp.bfloat16)] * count,
+        scratch_shapes=[pltpu.SemaphoreType.DMA((2 * count,))],
+        cost_estimate=pl.CostEstimate(flops=0, bytes_accessed=count << 19, transcendentals=0),
     )(*arrays)
 
 
@@ -166,14 +165,14 @@
     return rows_ref[at * 8 : at * 8 + 1, of_rows], rows_ref[at * 8 + 1 : at * 8 + 2, of_rows], sums_ref[cols(at), of_sums]
 
 
-def both_kernel(tile, bias_ref, query_ref, qc_sib, kv_a, kv_b, *states):
-    before, now = states[:-2], states[-2:]
+def both_kernel(tile, count, bias_ref, query_ref, qc_sib, *refs):
+    blocks, before, now = refs[:count], refs[count:-2], refs[-2:]
     for at in range(PAIRS):
         at_cols = cols(at)
-        keys = jnp.concatenate([kv_a[:BLK, at_cols], kv_b[:BLK, at_cols]], axis=0)
-        values = jnp.concatenate([kv_a[BLK:, at_cols], kv_b[BLK:, at_cols]], axis=0)
+        keys = jnp.concatenate([block[:BLK, at_cols] for block in blocks], axis=0)
+        values = jnp.concatenate([block[BLK:, at_cols] for block in blocks], axis=0)
         queries = [query_ref[:, my_cols(at)], qc_sib[:BLK, at_cols]]
-        biases = [bias_ref[(tile + 2 * side) * BLK : (tile + 2 * side + 2) * BLK] for side in range(2)]
+        biases = [bias_ref[(tile + 2 * side) * BLK : (tile + 2 * side + count) * BLK] for side in range(2)]
         state = get_state(*before, at) if before else None
         put_state(*now, at, absorb(queries, keys, values, biases, state))
 
@@ -264,8 +263,9 @@
     )(*operands)
 
 
-def both(tile, bias, queries, qc_sib, kv_a, kv_b, state=()):
-    return in_vmem(functools.partial(both_kernel, tile), 4, STATE, bias, queries, qc_sib, kv_a, kv_b, *state)
+def both(tile, bias, queries, qc_sib, blocks, state=()):
+    kernel = functools.partial(both_kernel, tile, len(blocks))
+    return in_vmem(kernel, 2 * len(blocks), STATE, bias, queries, qc_sib, *blocks, *state)
 
 
 def last_sib(*operands):
@@ -324,19 +324,21 @@
     move = lambda value, pairs: lax.ppermute(value, AXES, pairs)
     gain = out_gain.reshape(1, -1)
 
-    kv_own, kv_send, qc_send = split_heads(key_rows, value_rows, queries, cotangent)
+    kv_own, kv_send = split_heads((0, 1), key_rows, value_rows)
     r1 = move(kv_own, onward)
     r2 = move(kv_send, outward)
     kv_sib = move(kv_send, siblings)
+    (qc_send,) = split_heads((1,), after(queries, kv_sib), cotangent)
     qc_sib = move(qc_send, siblings)
-    bias = masks(block_keep, document_ids, link_lists)
     r3 = move(after(kv_own, qc_sib), backward)
     r4 = move(after(kv_send, qc_sib), inward)
     r5 = move(r1, onward)
-    state = both(0, bias, queries, qc_sib, kv_own, kv_sib)
+    bias = masks(block_keep, after(document_ids, kv_sib), link_lists)
+    state = both(0, bias, queries, qc_sib, (kv_own, kv_sib))
     r6 = move(after(r2, *state), backward)
-    state = both(4, bias, queries, qc_sib, r1, r2, state)
-    state = both(8, bias, queries, qc_sib, r3, r4, state)
+    state = both(4, bias, queries, qc_sib, (r1, r2), state)
+    state = both(8, bias, queries, qc_sib, (r3,), state)
+    state = both(9, bias, queries, qc_sib, (r4,), state)
     att_sib, terms = last_sib(bias, qc_sib, r5, *state, gain)
     back = move(att_sib, siblings)
     out, terms = last_own(groups * shards, bias, queries, cotangent, r6, *state, gain, terms)

time: 72.3 us -> 71.2 us (0.985)
  waiting for transfers between devices: 22.4 us -> 17.2 us
  starting transfers between devices: 29.4 us -> 31.9 us
  Pallas kernels: 18.6 us -> 20.1 us
    ppermute x9, waiting for transfers between devices: 12 us -> 6.78 us  [local(): move = lambda value, pairs: lax.ppermute(value, AXES, pairs)]
    ppermute x9, starting transfers between devices: 15.6 us -> 18.1 us  [local(): move = lambda value, pairs: lax.ppermute(value, AXES, pairs)]
    pallas_call x6 -> x7, Pallas kernels: 12.8 us -> 14.4 us  [in_vmem(): pl.pallas_call(kernel, in_specs=[smem] * scalars + [vmem] * (len(operands...]
    pallas_call x1 -> x2, Pallas kernels: 2.39 us -> 2.29 us  [split_heads(): pl.pallas_call(functools.partial(split_kernel, sides, 2), in_specs=[pl.Bl...]
  transfers between devices with their start and end apart: 10 -> 10, of which waited for: 4 -> 6; matrix products, arithmetic and copies ran while one was open for 0% -> 0% of each run, Pallas kernels for 22% -> 26%
where the time goes in v1:
time: 71.2 us; the launch traced here: 70.8 us
  starting transfers between devices  31.9 us (45%)
  Pallas kernels  20.1 us (28%)
  waiting for transfers between devices  17.2 us (24%)
  local copies, waits for them, and re-layouts  0.81 us (1%)
  between operations  0.81 us (1%)
    ppermute x9, starting transfers between devices, local(): move = lambda value, pairs: lax.ppermute(value, AXES, pairs)  18.1 us
    pallas_call x7, Pallas kernels, in_vmem(): pl.pallas_call(kernel, in_specs=[smem] * scalars + [vmem] * (len(operands...  14.4 us
    all_to_all x1, starting transfers between devices, local(): lax.all_to_all(terms.reshape(groups * shards, 1, BLK), AXES, 0, 0, tiled=...  13.8 us
    all_to_all x1, waiting for transfers between devices, local(): lax.all_to_all(terms.reshape(groups * shards, 1, BLK), AXES, 0, 0, tiled=...  10.4 us
    ppermute x9, waiting for transfers between devices, local(): move = lambda value, pairs: lax.ppermute(value, AXES, pairs)  6.78 us
    pallas_call x2, Pallas kernels, split_heads(): pl.pallas_call(functools.partial(split_kernel, sides, 2), in_specs=[pl.Bl...  2.29 us
    pallas_call x1, Pallas kernels, last_own(): pl.pallas_call(own_kernel, in_specs=[pl.BlockSpec(memory_space=pltpu.VMEM...  1.7 us
    pallas_call x1, Pallas kernels, fill_heads(): pl.pallas_call(fill_kernel, in_specs=[pl.BlockSpec(memory_space=pltpu.VME...  1.66 us
  transfers between devices with their start and end apart: 10, of which 6 were waited for; matrix products, arithmetic and copies ran while one was open for 0% of the time, Pallas kernels for 26%

profile of v1, /device:TPU:1, one launch (start us, length us, event | category | flops | bytes accessed | tf_op | source)
XLA Modules:
  0.0 70.8 jit_solution(2672938684489537516)
XLA Ops:
  0.6 1.2 %shard_map.95 = (bf16[256,1024]{1,0:T(8,128)(2,1)S(1)}, bf16[256,1024]{1,0:T(8,128)(2,1)S(1)}) custom-call(bf16[128,2048]{1,0:T(8,128)(2,1)} %refs_0_.1, bf16[128,2048]{1,0:T(8,128)(2,1)} %refs_1_.2), custom_call_target="tpu_custom_call" | custom-call | bytes 1048576 | tf_op jit(solution)/shard_map/pallas_call | solution.py:38
  1.9 3.3 %collective-permute-start = (bf16[256,1024]{1,0:T(8,128)(2,1)S(1)}, bf16[256,1024]{1,0:T(8,128)(2,1)S(1)}, u32[]{:S(2)}, u32[]{:S(2)}) collective-permute-start(bf16[256,1024]{1,0:T(8,128)(2,1)S(1)} %get-tuple-element.26), channel_id=1, source_target_pairs={{0,1},{1,0},{2,3},{3,2},{4,5},{5,4},{6,7},{7,6},{8,9},{9,8},{10,11... | collective-permute-start | bytes 1572872 | tf_op jit(solution)/shard_map/ppermute | solution.py:324
  5.2 1.5 %collective-permute-done.refs_1_ = bf16[256,1024]{1,0:T(8,128)(2,1)S(1)} collective-permute-done((bf16[256,1024]{1,0:T(8,128)(2,1)S(1)}, bf16[256,1024]{1,0:T(8,128)(2,1)S(1)}, u32[]{:S(2)}, u32[]{:S(2)}) %collective-permute-start) | collective-permute-done | bytes 524320 | tf_op jit(solution)/shard_map/ppermute | solution.py:324
  6.8 1.1 %shard_map.97 = bf16[256,1024]{1,0:T(8,128)(2,1)S(1)} custom-call(bf16[128,2048]{1,0:T(8,128)(2,1)} %query_ref.9, bf16[128,2048]{1,0:T(8,128)(2,1)} %cotangent_ref.1), custom_call_target="tpu_custom_call" | custom-call | bytes 524288 | tf_op jit(solution)/shard_map/pallas_call | solution.py:38
  8.3 1.9 %collective-permute-start.6 = (bf16[256,1024]{1,0:T(8,128)(2,1)}, bf16[256,1024]{1,0:T(8,128)(2,1)S(1)}, u32[]{:S(2)}, u32[]{:S(2)}) collective-permute-start(bf16[256,1024]{1,0:T(8,128)(2,1)} %copy-done.5), channel_id=1, source_target_pairs={{0,0},{1,2},{2,1},{3,4},{4,3},{5,6},{6,5},{7,8},{8,7},{9,10},{10,9... | collective-permute-start | bytes 1572872 | tf_op jit(solution)/shard_map/ppermute | solution.py:324
  10.3 1.0 %collective-permute-done.2.refs_0_ = bf16[256,1024]{1,0:T(8,128)(2,1)} collective-permute-done((bf16[256,1024]{1,0:T(8,128)(2,1)S(1)}, bf16[256,1024]{1,0:T(8,128)(2,1)}, u32[]{:S(2)}, u32[]{:S(2)}) %collective-permute-start.2) | collective-permute-done | bytes 524320 | tf_op jit(solution)/shard_map/ppermute | solution.py:324
  11.3 2.3 %collective-permute-start.3 = (bf16[256,1024]{1,0:T(8,128)(2,1)}, bf16[256,1024]{1,0:T(8,128)(2,1)S(1)}, u32[]{:S(2)}, u32[]{:S(2)}) collective-permute-start(bf16[256,1024]{1,0:T(8,128)(2,1)} %collective-permute-done.2.refs_0_), channel_id=1, source_target_pairs={{0,1},{1,3},{2,0},{3,5},{4,2},{5,7},{6,4},{7,9},{8,6},{9,11},{10,8... | collective-permute-start | bytes 1572872 | tf_op jit(solution)/shard_map/ppermute | solution.py:324
  13.7 1.0 %collective-permute-start.5 = (bf16[256,1024]{1,0:T(8,128)(2,1)S(1)}, bf16[256,1024]{1,0:T(8,128)(2,1)S(1)}, u32[]{:S(2)}, u32[]{:S(2)}) collective-permute-start(bf16[256,1024]{1,0:T(8,128)(2,1)S(1)} %get-tuple-element.27.refs_0_), channel_id=1, source_target_pairs={{1,0},{3,1},{0,2},{5,3},{2,4},{7,5},{4,6},{9,7},{6,8},{11,9},{8,10... | collective-permute-start | bytes 1572872 | tf_op jit(solution)/shard_map/ppermute | solution.py:324
  14.6 1.4 %shard_map.96.bias_ref = f32[1792,128]{1,0:T(8,128)S(1)} custom-call(s32[1,32,32]{2,1,0:T(8,128)S(1)} %copy-done.3, s32[1,4096]{1,0:T(1,128)S(1)} %copy-done.4, s32[1,32,8]{2,1,0:T(8,128)S(1)} %copy.12.links_ref), custom_call_target="tpu_custom_call" | custom-call | flops 67108864 | bytes 1048576 | tf_op jit(solution)/shard_map/pallas_call | solution.py:256
  16.0 1.7 %collective-permute-start.4 = (bf16[256,1024]{1,0:T(8,128)(2,1)}, bf16[256,1024]{1,0:T(8,128)(2,1)S(1)}, u32[]{:S(2)}, u32[]{:S(2)}) collective-permute-start(bf16[256,1024]{1,0:T(8,128)(2,1)} %copy-done.5), channel_id=1, source_target_pairs={{1,1},{3,0},{0,3},{5,2},{2,5},{7,4},{4,7},{9,6},{6,9},{11,8},{8,11... | collective-permute-start | bytes 1572872 | tf_op jit(solution)/shard_map/ppermute | solution.py:324
  17.7 2.9 %shard_map.98 = (f32[64,512]{1,0:T(8,128)S(1)}, f32[1024,256]{1,0:T(8,128)S(1)}) custom-call(f32[1792,128]{1,0:T(8,128)S(1)} %shard_map.96.bias_ref, bf16[128,2048]{1,0:T(8,128)(2,1)S(1)} %copy-done, bf16[256,1024]{1,0:T(8,128)(2,1)S(1)} %collective-permute-done.1.qc_sib.qc, bf16[256,1024]{1,0:T(8,128)(2,1)S(1)} %get-tuple-element.27.refs_0_, ...), custom_call_target="tpu_custom_call" | custom-call | flops 268435456 | bytes 1048576 | tf_op jit(solution)/shard_map/pallas_call | solution.py:256
  20.6 2.1 %collective-permute-done.6.refs_1_ = bf16[256,1024]{1,0:T(8,128)(2,1)S(1)} collective-permute-done((bf16[256,1024]{1,0:T(8,128)(2,1)}, bf16[256,1024]{1,0:T(8,128)(2,1)S(1)}, u32[]{:S(2)}, u32[]{:S(2)}) %collective-permute-start.6) | collective-permute-done | bytes 524320 | tf_op jit(solution)/shard_map/ppermute | solution.py:324
  23.1 4.0 %shard_map.99 = (f32[64,512]{1,0:T(8,128)S(1)}, f32[1024,256]{1,0:T(8,128)S(1)}) custom-call(f32[1792,128]{1,0:T(8,128)S(1)} %shard_map.96.bias_ref, bf16[128,2048]{1,0:T(8,128)(2,1)S(1)} %copy-done, bf16[256,1024]{1,0:T(8,128)(2,1)S(1)} %collective-permute-done.1.qc_sib.qc, bf16[256,1024]{1,0:T(8,128)(2,1)} %collective-permute-done.2.refs_0_, ...), custom_call_target="tpu_custom_call" | custom-call | flops 268435456 | bytes 1048576 | tf_op jit(solution)/shard_map/pallas_call | solution.py:256
  27.7 2.3 %shard_map.100 = (f32[64,512]{1,0:T(8,128)S(1)}, f32[1024,256]{1,0:T(8,128)S(1)}) custom-call(f32[1792,128]{1,0:T(8,128)S(1)} %shard_map.96.bias_ref, bf16[128,2048]{1,0:T(8,128)(2,1)S(1)} %copy-done, bf16[256,1024]{1,0:T(8,128)(2,1)S(1)} %collective-permute-done.1.qc_sib.qc, bf16[256,1024]{1,0:T(8,128)(2,1)S(1)} %collective-permute-done.5.refs_0_, ...), custom_call_target="tpu_custom_call" | custom-call | flops 134217728 | bytes 1048576 | tf_op jit(solution)/shard_map/pallas_call | solution.py:256
  30.1 2.3 %shard_map.101 = (f32[64,512]{1,0:T(8,128)S(1)}, f32[1024,256]{1,0:T(8,128)S(1)}) custom-call(f32[1792,128]{1,0:T(8,128)S(1)} %shard_map.96.bias_ref, bf16[128,2048]{1,0:T(8,128)(2,1)S(1)} %copy-done, bf16[256,1024]{1,0:T(8,128)(2,1)S(1)} %collective-permute-done.1.qc_sib.qc, bf16[256,1024]{1,0:T(8,128)(2,1)S(1)} %collective-permute-done.4.refs_0_, ...), custom_call_target="tpu_custom_call" | custom-call | flops 134217728 | bytes 1048576 | tf_op jit(solution)/shard_map/pallas_call | solution.py:256
  32.5 0.9 %shard_map.102 = (bf16[128,1024]{1,0:T(8,128)(2,1)S(1)}, f32[8,128]{1,0:T(8,128)S(1)}) custom-call(f32[1792,128]{1,0:T(8,128)S(1)} %shard_map.96.bias_ref, bf16[256,1024]{1,0:T(8,128)(2,1)S(1)} %collective-permute-done.1.qc_sib.qc, bf16[256,1024]{1,0:T(8,128)(2,1)S(1)} %collective-permute-done.3.kv, f32[64,512]{1,0:T(8,128)S(1)} %get-tuple-element.34.rows, ...), custom_call_target="tpu_custom_call" | custom-call | flops 67108864 | bytes 1048576 | tf_op jit(solution)/shard_map/pallas_call | solution.py:256
  33.4 7.0 %collective-permute-start.7 = (bf16[128,1024]{1,0:T(8,128)(2,1)S(1)}, bf16[128,1024]{1,0:T(8,128)(2,1)S(1)}, u32[]{:S(2)}, u32[]{:S(2)}) collective-permute-start(bf16[128,1024]{1,0:T(8,128)(2,1)S(1)} %get-tuple-element.36), channel_id=1, source_target_pairs={{0,1},{1,0},{2,3},{3,2},{4,5},{5,4},{6,7},{7,6},{8,9},{9,8},{10,11... | collective-permute-start | bytes 786440 | tf_op jit(solution)/shard_map/ppermute | solution.py:324
  40.4 1.5 %collective-permute-done.8.kv = bf16[256,1024]{1,0:T(8,128)(2,1)S(1)} collective-permute-done((bf16[256,1024]{1,0:T(8,128)(2,1)S(1)}, bf16[256,1024]{1,0:T(8,128)(2,1)S(1)}, u32[]{:S(2)}, u32[]{:S(2)}) %collective-permute-start.8) | collective-permute-done | bytes 524320 | tf_op jit(solution)/shard_map/ppermute | solution.py:324
  41.9 1.7 %shard_map.103 = (bf16[128,2048]{1,0:T(8,128)(2,1)}, f32[256,128]{1,0:T(8,128)}) custom-call(f32[1792,128]{1,0:T(8,128)S(1)} %shard_map.96.bias_ref, bf16[128,2048]{1,0:T(8,128)(2,1)S(1)} %copy-done, bf16[128,2048]{1,0:T(8,128)(2,1)S(1)} %copy-done.1, bf16[256,1024]{1,0:T(8,128)(2,1)S(1)} %collective-permute-done.8.kv, ...), custom_call_target="tpu_custom_call" | custom-call | flops 67108864 | bytes 1048576 | tf_op jit(solution)/shard_map/pallas_call | solution.py:277
  43.6 13.8 %all-to-all-start = ((f32[256,1,128]{2,1,0:T(1,128)}), f32[256,1,128]{2,1,0:T(1,128)S(1)}, u32[]{:S(2)}, u32[]{:S(2)}) async-start(f32[256,1,128]{2,1,0:T(1,128)} %bitcast.2), calls=%async_computation | async-start | bytes 262144 | tf_op jit(solution)/shard_map/all_to_all | solution.py:345
  57.4 0.7 copy-done.6
  58.1 1.7 %shard_map.104 = bf16[128,2048]{1,0:T(8,128)(2,1)} custom-call(bf16[128,1024]{1,0:T(8,128)(2,1)} %copy-done.6, bf16[128,2048]{1,0:T(8,128)(2,1)} %get-tuple-element.39.out_in), custom_call_target="tpu_custom_call", output_to_operand_aliasing={{}: (1, {})} | custom-call | bytes 1048576 | tf_op jit(solution)/shard_map/pallas_call | solution.py:236
  59.8 10.4 %all-to-all-done = f32[256,1,128]{2,1,0:T(1,128)S(1)} async-done(((f32[256,1,128]{2,1,0:T(1,128)}), f32[256,1,128]{2,1,0:T(1,128)S(1)}, u32[]{:S(2)}, u32[]{:S(2)}) %all-to-all-start) | async-done | bytes 131104 | tf_op jit(solution)/shard_map/all_to_all | solution.py:345
  70.2 0.6 shard_map.105
  (24 shorter events, 1.6 us)
Async XLA Ops:
  1.9 4.9 %copy-start.5 = (bf16[256,1024]{1,0:T(8,128)(2,1)}, bf16[256,1024]{1,0:T(8,128)(2,1)S(1)}, u32[]{:S(2)}) copy-start(bf16[256,1024]{1,0:T(8,128)(2,1)S(1)} %get-tuple-element.26) | copy-start | bytes 1572868
  1.9 4.9 %collective-permute-start = (bf16[256,1024]{1,0:T(8,128)(2,1)S(1)}, bf16[256,1024]{1,0:T(8,128)(2,1)S(1)}, u32[]{:S(2)}, u32[]{:S(2)}) collective-permute-start(bf16[256,1024]{1,0:T(8,128)(2,1)S(1)} %get-tuple-element.26), channel_id=1, source_target_pairs={{0,1},{1,0},{2,3},{3,2},{4,5},{5,4},{6,7},{7,6},{8,9},{9,8},{10,11... | collective-permute-start | bytes 1572872 | tf_op jit(solution)/shard_map/ppermute | solution.py:324
  5.2 5.0 %copy-start.7 = (s32[1,32,8]{1,2,0:T(8,128)S(1)}, s32[1,32,8]{1,2,0:T(8,128)}, u32[]{:S(2)}) copy-start(s32[1,32,8]{1,2,0:T(8,128)} %param.12) | copy-start | bytes 3076
  5.2 6.1 %collective-permute-start.2 = (bf16[256,1024]{1,0:T(8,128)(2,1)S(1)}, bf16[256,1024]{1,0:T(8,128)(2,1)}, u32[]{:S(2)}, u32[]{:S(2)}) collective-permute-start(bf16[256,1024]{1,0:T(8,128)(2,1)S(1)} %get-tuple-element.27.refs_0_), channel_id=1, source_target_pairs={{0,1},{1,3},{2,0},{3,5},{4,2},{5,7},{6,4},{7,9},{8,6},{9,11},{10,8... | collective-permute-start | bytes 1572872 | tf_op jit(solution)/shard_map/ppermute | solution.py:324
  6.8 7.9 %copy-start.3 = (s32[1,32,32]{2,1,0:T(8,128)S(1)}, s32[1,32,32]{2,1,0:T(8,128)}, u32[]{:S(2)}) copy-start(s32[1,32,32]{2,1,0:T(8,128)} %keep_ref.1) | copy-start | bytes 12292
  6.8 7.9 %copy-start.4 = (s32[1,4096]{1,0:T(1,128)S(1)}, s32[1,4096]{1,0:T(1,128)}, u32[]{:S(2)}) copy-start(s32[1,4096]{1,0:T(1,128)} %docs_ref) | copy-start | bytes 49156
  7.8 9.9 %copy-start = (bf16[128,2048]{1,0:T(8,128)(2,1)S(1)}, bf16[128,2048]{1,0:T(8,128)(2,1)}, u32[]{:S(2)}) copy-start(bf16[128,2048]{1,0:T(8,128)(2,1)} %query_ref.9) | copy-start | bytes 1572868
  7.8 5.8 %collective-permute-start.1 = (bf16[256,1024]{1,0:T(8,128)(2,1)S(1)}, bf16[256,1024]{1,0:T(8,128)(2,1)S(1)}, u32[]{:S(2)}, u32[]{:S(2)}) collective-permute-start(bf16[256,1024]{1,0:T(8,128)(2,1)S(1)} %shard_map.97), channel_id=1, source_target_pairs={{0,1},{1,0},{2,3},{3,2},{4,5},{5,4},{6,7},{7,6},{8,9},{9,8},{10,11... | collective-permute-start | bytes 1572872 | tf_op jit(solution)/shard_map/ppermute | solution.py:324
  8.3 14.4 %collective-permute-start.6 = (bf16[256,1024]{1,0:T(8,128)(2,1)}, bf16[256,1024]{1,0:T(8,128)(2,1)S(1)}, u32[]{:S(2)}, u32[]{:S(2)}) collective-permute-start(bf16[256,1024]{1,0:T(8,128)(2,1)} %copy-done.5), channel_id=1, source_target_pairs={{0,0},{1,2},{2,1},{3,4},{4,3},{5,6},{6,5},{7,8},{8,7},{9,10},{10,9... | collective-permute-start | bytes 1572872 | tf_op jit(solution)/shard_map/ppermute | solution.py:324
  11.3 21.1 %collective-permute-start.3 = (bf16[256,1024]{1,0:T(8,128)(2,1)}, bf16[256,1024]{1,0:T(8,128)(2,1)S(1)}, u32[]{:S(2)}, u32[]{:S(2)}) collective-permute-start(bf16[256,1024]{1,0:T(8,128)(2,1)} %collective-permute-done.2.refs_0_), channel_id=1, source_target_pairs={{0,1},{1,3},{2,0},{3,5},{4,2},{5,7},{6,4},{7,9},{8,6},{9,11},{10,8... | collective-permute-start | bytes 1572872 | tf_op jit(solution)/shard_map/ppermute | solution.py:324
  13.7 14.1 %collective-permute-start.5 = (bf16[256,1024]{1,0:T(8,128)(2,1)S(1)}, bf16[256,1024]{1,0:T(8,128)(2,1)S(1)}, u32[]{:S(2)}, u32[]{:S(2)}) collective-permute-start(bf16[256,1024]{1,0:T(8,128)(2,1)S(1)} %get-tuple-element.27.refs_0_), channel_id=1, source_target_pairs={{1,0},{3,1},{0,2},{5,3},{2,4},{7,5},{4,6},{9,7},{6,8},{11,9},{8,10... | collective-permute-start | bytes 1572872 | tf_op jit(solution)/shard_map/ppermute | solution.py:324
  16.0 14.1 %collective-permute-start.4 = (bf16[256,1024]{1,0:T(8,128)(2,1)}, bf16[256,1024]{1,0:T(8,128)(2,1)S(1)}, u32[]{:S(2)}, u32[]{:S(2)}) collective-permute-start(bf16[256,1024]{1,0:T(8,128)(2,1)} %copy-done.5), channel_id=1, source_target_pairs={{1,1},{3,0},{0,3},{5,2},{2,5},{7,4},{4,7},{9,6},{6,9},{11,8},{8,11... | collective-permute-start | bytes 1572872 | tf_op jit(solution)/shard_map/ppermute | solution.py:324
  22.7 19.2 %collective-permute-start.8 = (bf16[256,1024]{1,0:T(8,128)(2,1)S(1)}, bf16[256,1024]{1,0:T(8,128)(2,1)S(1)}, u32[]{:S(2)}, u32[]{:S(2)}) collective-permute-start(bf16[256,1024]{1,0:T(8,128)(2,1)S(1)} %collective-permute-done.6.refs_1_), channel_id=1, source_target_pairs={{1,0},{3,1},{0,2},{5,3},{2,4},{7,5},{4,6},{9,7},{6,8},{11,9},{8,10... | collective-permute-start | bytes 1572872 | tf_op jit(solution)/shard_map/ppermute | solution.py:324
  30.1 2.4 %copy-start.2 = (f32[2048]{0:T(1024)S(1)}, f32[2048]{0:T(1024)}, u32[]{:S(2)}) copy-start(f32[2048]{0:T(1024)} %param.14) | copy-start | bytes 24580
  32.5 9.5 %copy-start.1 = (bf16[128,2048]{1,0:T(8,128)(2,1)S(1)}, bf16[128,2048]{1,0:T(8,128)(2,1)}, u32[]{:S(2)}) copy-start(bf16[128,2048]{1,0:T(8,128)(2,1)} %cotangent_ref.1) | copy-start | bytes 1572868
  33.4 24.0 %collective-permute-start.7 = (bf16[128,1024]{1,0:T(8,128)(2,1)S(1)}, bf16[128,1024]{1,0:T(8,128)(2,1)S(1)}, u32[]{:S(2)}, u32[]{:S(2)}) collective-permute-start(bf16[128,1024]{1,0:T(8,128)(2,1)S(1)} %get-tuple-element.36), channel_id=1, source_target_pairs={{0,1},{1,0},{2,3},{3,2},{4,5},{5,4},{6,7},{7,6},{8,9},{9,8},{10,11... | collective-permute-start | bytes 786440 | tf_op jit(solution)/shard_map/ppermute | solution.py:324
  43.6 26.6 %all-to-all-start = ((f32[256,1,128]{2,1,0:T(1,128)}), f32[256,1,128]{2,1,0:T(1,128)S(1)}, u32[]{:S(2)}, u32[]{:S(2)}) async-start(f32[256,1,128]{2,1,0:T(1,128)} %bitcast.2), calls=%async_computation | async-start | bytes 262144 | tf_op jit(solution)/shard_map/all_to_all | solution.py:345
  57.4 0.7 copy-start.6

commit v2 on v1

--- a/solution.py
+++ b/solution.py
@@ -14,6 +14,7 @@
 BLK = 128
 HALF = HEADS * HDIM // 2
 PAIRS = HALF // 128
+SENT_AFTER = (3, 6, 8)
 NEGATIVE_FILL = -1e30
 AXES = ("dp", "seq")
 
@@ -178,7 +179,7 @@
 
 
 def finish(state, gain, cotangent):
-    mixed = jnp.transpose(state[2] / spread(state[1]))
+    mixed = jnp.transpose(state[2] * spread(1.0 / state[1]))
     attended = (gain * mixed).astype(jnp.bfloat16)
     terms = jnp.sum(mixed * cotangent.astype(jnp.float32), axis=0, keepdims=True)
     return attended, terms
@@ -210,16 +211,23 @@
         copies[-1].start()
 
     half = PAIRS * devices
-    here = pl.ds(pl.multiple_of((1 - core) * half, half), half)
-    spread_terms[here] = jnp.zeros((half, BLK), jnp.float32)
-    send(spread_terms.at[here], terms_ref.at[here])
+    there = pl.ds(pl.multiple_of((1 - core) * half, half), half)
+    spread_terms[there] = jnp.zeros((half, BLK), jnp.float32)
+    send(spread_terms.at[there], terms_ref.at[there])
+    sent = 0
     for at in range(PAIRS):
         query, cotangent = query_ref[:, my_cols(at)], cotangent_ref[:, my_cols(at)]
         att[:, cols(at)], terms = last(13, 0, at, bias_ref, query, cotangent, kv, rows, sums, gain_ref)
-        send(att.at[:, cols(at)], out_ref.at[:, my_cols(at)])
         here = pl.ds(pl.multiple_of((core * PAIRS + at) * devices, devices), devices)
         spread_terms[here] = jnp.broadcast_to(terms + terms_in[at : at + 1], (devices, BLK))
-        send(spread_terms.at[here], terms_ref.at[here])
+        if at + 1 in SENT_AFTER:
+            width = (at + 1 - sent) * BLK
+            columns = pl.ds(pl.multiple_of(core * HALF + sent * BLK, BLK), width)
+            send(att.at[:, sent * BLK : (at + 1) * BLK], out_ref.at[:, columns])
+            place = (core * PAIRS + sent) * devices
+            here = pl.ds(pl.multiple_of(place, devices), (at + 1 - sent) * devices)
+            send(spread_terms.at[here], terms_ref.at[here])
+            sent = at + 1
     for copy in copies:
         copy.wait()
 
@@ -285,7 +293,7 @@
         scratch_shapes=[
             pltpu.VMEM((BLK, HALF), jnp.bfloat16),
             pltpu.VMEM((devices, BLK), jnp.float32),
-            pltpu.SemaphoreType.DMA((1 + 2 * PAIRS,)),
+            pltpu.SemaphoreType.DMA((1 + 2 * len(SENT_AFTER),)),
         ],
         cost_estimate=pl.CostEstimate(flops=64 * BLK * BLK * HDIM, bytes_accessed=1 << 20, transcendentals=16 * BLK * BLK),
         compiler_params=pltpu.CompilerParams(vmem_limit_bytes=8 << 20),

time: 71.2 us -> 71.1 us (level)
  no operation moved by 1% of the time
where the time goes in v2:
time: 71.1 us; the launch traced here: 70.7 us
  starting transfers between devices  31.9 us (45%)
  Pallas kernels  20 us (28%)
  waiting for transfers between devices  17.2 us (24%)
  local copies, waits for them, and re-layouts  0.81 us (1%)
  between operations  0.81 us (1%)
    ppermute x9, starting transfers between devices, local(): move = lambda value, pairs: lax.ppermute(value, AXES, pairs)  18.1 us
    pallas_call x7, Pallas kernels, in_vmem(): pl.pallas_call(kernel, in_specs=[smem] * scalars + [vmem] * (len(operands...  14.4 us
    all_to_all x1, starting transfers between devices, local(): lax.all_to_all(terms.reshape(groups * shards, 1, BLK), AXES, 0, 0, tiled=...  13.8 us
    all_to_all x1, waiting for transfers between devices, local(): lax.all_to_all(terms.reshape(groups * shards, 1, BLK), AXES, 0, 0, tiled=...  10.4 us
    ppermute x9, waiting for transfers between devices, local(): move = lambda value, pairs: lax.ppermute(value, AXES, pairs)  6.79 us
    pallas_call x2, Pallas kernels, split_heads(): pl.pallas_call(functools.partial(split_kernel, sides, 2), in_specs=[pl.Bl...  2.29 us
    pallas_call x1, Pallas kernels, fill_heads(): pl.pallas_call(fill_kernel, in_specs=[pl.BlockSpec(memory_space=pltpu.VME...  1.66 us
    pallas_call x1, Pallas kernels, last_own(): pl.pallas_call(own_kernel, in_specs=[pl.BlockSpec(memory_space=pltpu.VMEM...  1.61 us
  transfers between devices with their start and end apart: 10, of which 6 were waited for; matrix products, arithmetic and copies ran while one was open for 0% of the time, Pallas kernels for 26%

profile of v2, /device:TPU:1, one launch (start us, length us, event | category | flops | bytes accessed | tf_op | source)
XLA Modules:
  0.0 70.7 jit_solution(4046907793945706722)
XLA Ops:
  0.6 1.2 %shard_map.95 = (bf16[256,1024]{1,0:T(8,128)(2,1)S(1)}, bf16[256,1024]{1,0:T(8,128)(2,1)S(1)}) custom-call(bf16[128,2048]{1,0:T(8,128)(2,1)} %refs_0_.1, bf16[128,2048]{1,0:T(8,128)(2,1)} %refs_1_.2), custom_call_target="tpu_custom_call" | custom-call | bytes 1048576 | tf_op jit(solution)/shard_map/pallas_call | solution.py:39
  1.9 3.3 %collective-permute-start = (bf16[256,1024]{1,0:T(8,128)(2,1)S(1)}, bf16[256,1024]{1,0:T(8,128)(2,1)S(1)}, u32[]{:S(2)}, u32[]{:S(2)}) collective-permute-start(bf16[256,1024]{1,0:T(8,128)(2,1)S(1)} %get-tuple-element.26), channel_id=1, source_target_pairs={{0,1},{1,0},{2,3},{3,2},{4,5},{5,4},{6,7},{7,6},{8,9},{9,8},{10,11... | collective-permute-start | bytes 1572872 | tf_op jit(solution)/shard_map/ppermute | solution.py:332
  5.2 1.5 %collective-permute-done.refs_1_ = bf16[256,1024]{1,0:T(8,128)(2,1)S(1)} collective-permute-done((bf16[256,1024]{1,0:T(8,128)(2,1)S(1)}, bf16[256,1024]{1,0:T(8,128)(2,1)S(1)}, u32[]{:S(2)}, u32[]{:S(2)}) %collective-permute-start) | collective-permute-done | bytes 524320 | tf_op jit(solution)/shard_map/ppermute | solution.py:332
  6.8 1.1 %shard_map.97 = bf16[256,1024]{1,0:T(8,128)(2,1)S(1)} custom-call(bf16[128,2048]{1,0:T(8,128)(2,1)} %query_ref.9, bf16[128,2048]{1,0:T(8,128)(2,1)} %cotangent_ref.1), custom_call_target="tpu_custom_call" | custom-call | bytes 524288 | tf_op jit(solution)/shard_map/pallas_call | solution.py:39
  8.3 1.9 %collective-permute-start.6 = (bf16[256,1024]{1,0:T(8,128)(2,1)}, bf16[256,1024]{1,0:T(8,128)(2,1)S(1)}, u32[]{:S(2)}, u32[]{:S(2)}) collective-permute-start(bf16[256,1024]{1,0:T(8,128)(2,1)} %copy-done.5), channel_id=1, source_target_pairs={{0,0},{1,2},{2,1},{3,4},{4,3},{5,6},{6,5},{7,8},{8,7},{9,10},{10,9... | collective-permute-start | bytes 1572872 | tf_op jit(solution)/shard_map/ppermute | solution.py:332
  10.3 1.0 %collective-permute-done.2.refs_0_ = bf16[256,1024]{1,0:T(8,128)(2,1)} collective-permute-done((bf16[256,1024]{1,0:T(8,128)(2,1)S(1)}, bf16[256,1024]{1,0:T(8,128)(2,1)}, u32[]{:S(2)}, u32[]{:S(2)}) %collective-permute-start.2) | collective-permute-done | bytes 524320 | tf_op jit(solution)/shard_map/ppermute | solution.py:332
  11.3 2.3 %collective-permute-start.3 = (bf16[256,1024]{1,0:T(8,128)(2,1)}, bf16[256,1024]{1,0:T(8,128)(2,1)S(1)}, u32[]{:S(2)}, u32[]{:S(2)}) collective-permute-start(bf16[256,1024]{1,0:T(8,128)(2,1)} %collective-permute-done.2.refs_0_), channel_id=1, source_target_pairs={{0,1},{1,3},{2,0},{3,5},{4,2},{5,7},{6,4},{7,9},{8,6},{9,11},{10,8... | collective-permute-start | bytes 1572872 | tf_op jit(solution)/shard_map/ppermute | solution.py:332
  13.7 1.0 %collective-permute-start.5 = (bf16[256,1024]{1,0:T(8,128)(2,1)S(1)}, bf16[256,1024]{1,0:T(8,128)(2,1)S(1)}, u32[]{:S(2)}, u32[]{:S(2)}) collective-permute-start(bf16[256,1024]{1,0:T(8,128)(2,1)S(1)} %get-tuple-element.27.refs_0_), channel_id=1, source_target_pairs={{1,0},{3,1},{0,2},{5,3},{2,4},{7,5},{4,6},{9,7},{6,8},{11,9},{8,10... | collective-permute-start | bytes 1572872 | tf_op jit(solution)/shard_map/ppermute | solution.py:332
  14.6 1.4 %shard_map.96.bias_ref = f32[1792,128]{1,0:T(8,128)S(1)} custom-call(s32[1,32,32]{2,1,0:T(8,128)S(1)} %copy-done.3, s32[1,4096]{1,0:T(1,128)S(1)} %copy-done.4, s32[1,32,8]{2,1,0:T(8,128)S(1)} %copy.12.links_ref), custom_call_target="tpu_custom_call" | custom-call | flops 67108864 | bytes 1048576 | tf_op jit(solution)/shard_map/pallas_call | solution.py:264
  16.0 1.7 %collective-permute-start.4 = (bf16[256,1024]{1,0:T(8,128)(2,1)}, bf16[256,1024]{1,0:T(8,128)(2,1)S(1)}, u32[]{:S(2)}, u32[]{:S(2)}) collective-permute-start(bf16[256,1024]{1,0:T(8,128)(2,1)} %copy-done.5), channel_id=1, source_target_pairs={{1,1},{3,0},{0,3},{5,2},{2,5},{7,4},{4,7},{9,6},{6,9},{11,8},{8,11... | collective-permute-start | bytes 1572872 | tf_op jit(solution)/shard_map/ppermute | solution.py:332
  17.7 2.9 %shard_map.98 = (f32[64,512]{1,0:T(8,128)S(1)}, f32[1024,256]{1,0:T(8,128)S(1)}) custom-call(f32[1792,128]{1,0:T(8,128)S(1)} %shard_map.96.bias_ref, bf16[128,2048]{1,0:T(8,128)(2,1)S(1)} %copy-done, bf16[256,1024]{1,0:T(8,128)(2,1)S(1)} %collective-permute-done.1.qc_sib.qc, bf16[256,1024]{1,0:T(8,128)(2,1)S(1)} %get-tuple-element.27.refs_0_, ...), custom_call_target="tpu_custom_call" | custom-call | flops 268435456 | bytes 1048576 | tf_op jit(solution)/shard_map/pallas_call | solution.py:264
  20.6 2.1 %collective-permute-done.6.refs_1_ = bf16[256,1024]{1,0:T(8,128)(2,1)S(1)} collective-permute-done((bf16[256,1024]{1,0:T(8,128)(2,1)}, bf16[256,1024]{1,0:T(8,128)(2,1)S(1)}, u32[]{:S(2)}, u32[]{:S(2)}) %collective-permute-start.6) | collective-permute-done | bytes 524320 | tf_op jit(solution)/shard_map/ppermute | solution.py:332
  23.1 4.0 %shard_map.99 = (f32[64,512]{1,0:T(8,128)S(1)}, f32[1024,256]{1,0:T(8,128)S(1)}) custom-call(f32[1792,128]{1,0:T(8,128)S(1)} %shard_map.96.bias_ref, bf16[128,2048]{1,0:T(8,128)(2,1)S(1)} %copy-done, bf16[256,1024]{1,0:T(8,128)(2,1)S(1)} %collective-permute-done.1.qc_sib.qc, bf16[256,1024]{1,0:T(8,128)(2,1)} %collective-permute-done.2.refs_0_, ...), custom_call_target="tpu_custom_call" | custom-call | flops 268435456 | bytes 1048576 | tf_op jit(solution)/shard_map/pallas_call | solution.py:264
  27.7 2.3 %shard_map.100 = (f32[64,512]{1,0:T(8,128)S(1)}, f32[1024,256]{1,0:T(8,128)S(1)}) custom-call(f32[1792,128]{1,0:T(8,128)S(1)} %shard_map.96.bias_ref, bf16[128,2048]{1,0:T(8,128)(2,1)S(1)} %copy-done, bf16[256,1024]{1,0:T(8,128)(2,1)S(1)} %collective-permute-done.1.qc_sib.qc, bf16[256,1024]{1,0:T(8,128)(2,1)S(1)} %collective-permute-done.5.refs_0_, ...), custom_call_target="tpu_custom_call" | custom-call | flops 134217728 | bytes 1048576 | tf_op jit(solution)/shard_map/pallas_call | solution.py:264
  30.1 2.3 %shard_map.101 = (f32[64,512]{1,0:T(8,128)S(1)}, f32[1024,256]{1,0:T(8,128)S(1)}) custom-call(f32[1792,128]{1,0:T(8,128)S(1)} %shard_map.96.bias_ref, bf16[128,2048]{1,0:T(8,128)(2,1)S(1)} %copy-done, bf16[256,1024]{1,0:T(8,128)(2,1)S(1)} %collective-permute-done.1.qc_sib.qc, bf16[256,1024]{1,0:T(8,128)(2,1)S(1)} %collective-permute-done.4.refs_0_, ...), custom_call_target="tpu_custom_call" | custom-call | flops 134217728 | bytes 1048576 | tf_op jit(solution)/shard_map/pallas_call | solution.py:264
  32.5 0.9 %shard_map.102 = (bf16[128,1024]{1,0:T(8,128)(2,1)S(1)}, f32[8,128]{1,0:T(8,128)S(1)}) custom-call(f32[1792,128]{1,0:T(8,128)S(1)} %shard_map.96.bias_ref, bf16[256,1024]{1,0:T(8,128)(2,1)S(1)} %collective-permute-done.1.qc_sib.qc, bf16[256,1024]{1,0:T(8,128)(2,1)S(1)} %collective-permute-done.3.kv, f32[64,512]{1,0:T(8,128)S(1)} %get-tuple-element.34.rows, ...), custom_call_target="tpu_custom_call" | custom-call | flops 67108864 | bytes 1048576 | tf_op jit(solution)/shard_map/pallas_call | solution.py:264
  33.4 7.0 %collective-permute-start.7 = (bf16[128,1024]{1,0:T(8,128)(2,1)S(1)}, bf16[128,1024]{1,0:T(8,128)(2,1)S(1)}, u32[]{:S(2)}, u32[]{:S(2)}) collective-permute-start(bf16[128,1024]{1,0:T(8,128)(2,1)S(1)} %get-tuple-element.36), channel_id=1, source_target_pairs={{0,1},{1,0},{2,3},{3,2},{4,5},{5,4},{6,7},{7,6},{8,9},{9,8},{10,11... | collective-permute-start | bytes 786440 | tf_op jit(solution)/shard_map/ppermute | solution.py:332
  40.3 1.6 %collective-permute-done.8.kv = bf16[256,1024]{1,0:T(8,128)(2,1)S(1)} collective-permute-done((bf16[256,1024]{1,0:T(8,128)(2,1)S(1)}, bf16[256,1024]{1,0:T(8,128)(2,1)S(1)}, u32[]{:S(2)}, u32[]{:S(2)}) %collective-permute-start.8) | collective-permute-done | bytes 524320 | tf_op jit(solution)/shard_map/ppermute | solution.py:332
  41.9 1.6 %shard_map.103 = (bf16[128,2048]{1,0:T(8,128)(2,1)}, f32[256,128]{1,0:T(8,128)}) custom-call(f32[1792,128]{1,0:T(8,128)S(1)} %shard_map.96.bias_ref, bf16[128,2048]{1,0:T(8,128)(2,1)S(1)} %copy-done, bf16[128,2048]{1,0:T(8,128)(2,1)S(1)} %copy-done.1, bf16[256,1024]{1,0:T(8,128)(2,1)S(1)} %collective-permute-done.8.kv, ...), custom_call_target="tpu_custom_call" | custom-call | flops 67108864 | bytes 1048576 | tf_op jit(solution)/shard_map/pallas_call | solution.py:285
  43.5 13.8 %all-to-all-start = ((f32[256,1,128]{2,1,0:T(1,128)}), f32[256,1,128]{2,1,0:T(1,128)S(1)}, u32[]{:S(2)}, u32[]{:S(2)}) async-start(f32[256,1,128]{2,1,0:T(1,128)} %bitcast.2), calls=%async_computation | async-start | bytes 262144 | tf_op jit(solution)/shard_map/all_to_all | solution.py:353
  57.3 0.7 copy-done.6
  58.0 1.7 %shard_map.104 = bf16[128,2048]{1,0:T(8,128)(2,1)} custom-call(bf16[128,1024]{1,0:T(8,128)(2,1)} %copy-done.6, bf16[128,2048]{1,0:T(8,128)(2,1)} %get-tuple-element.39.out_in), custom_call_target="tpu_custom_call", output_to_operand_aliasing={{}: (1, {})} | custom-call | bytes 1048576 | tf_op jit(solution)/shard_map/pallas_call | solution.py:244
  59.7 10.4 %all-to-all-done = f32[256,1,128]{2,1,0:T(1,128)S(1)} async-done(((f32[256,1,128]{2,1,0:T(1,128)}), f32[256,1,128]{2,1,0:T(1,128)S(1)}, u32[]{:S(2)}, u32[]{:S(2)}) %all-to-all-start) | async-done | bytes 131104 | tf_op jit(solution)/shard_map/all_to_all | solution.py:353
  70.1 0.6 shard_map.105
  (24 shorter events, 1.6 us)
Async XLA Ops:
  1.9 4.9 %copy-start.5 = (bf16[256,1024]{1,0:T(8,128)(2,1)}, bf16[256,1024]{1,0:T(8,128)(2,1)S(1)}, u32[]{:S(2)}) copy-start(bf16[256,1024]{1,0:T(8,128)(2,1)S(1)} %get-tuple-element.26) | copy-start | bytes 1572868
  1.9 4.9 %collective-permute-start = (bf16[256,1024]{1,0:T(8,128)(2,1)S(1)}, bf16[256,1024]{1,0:T(8,128)(2,1)S(1)}, u32[]{:S(2)}, u32[]{:S(2)}) collective-permute-start(bf16[256,1024]{1,0:T(8,128)(2,1)S(1)} %get-tuple-element.26), channel_id=1, source_target_pairs={{0,1},{1,0},{2,3},{3,2},{4,5},{5,4},{6,7},{7,6},{8,9},{9,8},{10,11... | collective-permute-start | bytes 1572872 | tf_op jit(solution)/shard_map/ppermute | solution.py:332
  5.2 5.0 %copy-start.7 = (s32[1,32,8]{1,2,0:T(8,128)S(1)}, s32[1,32,8]{1,2,0:T(8,128)}, u32[]{:S(2)}) copy-start(s32[1,32,8]{1,2,0:T(8,128)} %param.12) | copy-start | bytes 3076
  5.2 6.1 %collective-permute-start.2 = (bf16[256,1024]{1,0:T(8,128)(2,1)S(1)}, bf16[256,1024]{1,0:T(8,128)(2,1)}, u32[]{:S(2)}, u32[]{:S(2)}) collective-permute-start(bf16[256,1024]{1,0:T(8,128)(2,1)S(1)} %get-tuple-element.27.refs_0_), channel_id=1, source_target_pairs={{0,1},{1,3},{2,0},{3,5},{4,2},{5,7},{6,4},{7,9},{8,6},{9,11},{10,8... | collective-permute-start | bytes 1572872 | tf_op jit(solution)/shard_map/ppermute | solution.py:332
  6.8 7.9 %copy-start.3 = (s32[1,32,32]{2,1,0:T(8,128)S(1)}, s32[1,32,32]{2,1,0:T(8,128)}, u32[]{:S(2)}) copy-start(s32[1,32,32]{2,1,0:T(8,128)} %keep_ref.1) | copy-start | bytes 12292
  6.8 7.9 %copy-start.4 = (s32[1,4096]{1,0:T(1,128)S(1)}, s32[1,4096]{1,0:T(1,128)}, u32[]{:S(2)}) copy-start(s32[1,4096]{1,0:T(1,128)} %docs_ref) | copy-start | bytes 49156
  7.8 9.9 %copy-start = (bf16[128,2048]{1,0:T(8,128)(2,1)S(1)}, bf16[128,2048]{1,0:T(8,128)(2,1)}, u32[]{:S(2)}) copy-start(bf16[128,2048]{1,0:T(8,128)(2,1)} %query_ref.9) | copy-start | bytes 1572868
  7.8 5.8 %collective-permute-start.1 = (bf16[256,1024]{1,0:T(8,128)(2,1)S(1)}, bf16[256,1024]{1,0:T(8,128)(2,1)S(1)}, u32[]{:S(2)}, u32[]{:S(2)}) collective-permute-start(bf16[256,1024]{1,0:T(8,128)(2,1)S(1)} %shard_map.97), channel_id=1, source_target_pairs={{0,1},{1,0},{2,3},{3,2},{4,5},{5,4},{6,7},{7,6},{8,9},{9,8},{10,11... | collective-permute-start | bytes 1572872 | tf_op jit(solution)/shard_map/ppermute | solution.py:332
  8.3 14.4 %collective-permute-start.6 = (bf16[256,1024]{1,0:T(8,128)(2,1)}, bf16[256,1024]{1,0:T(8,128)(2,1)S(1)}, u32[]{:S(2)}, u32[]{:S(2)}) collective-permute-start(bf16[256,1024]{1,0:T(8,128)(2,1)} %copy-done.5), channel_id=1, source_target_pairs={{0,0},{1,2},{2,1},{3,4},{4,3},{5,6},{6,5},{7,8},{8,7},{9,10},{10,9... | collective-permute-start | bytes 1572872 | tf_op jit(solution)/shard_map/ppermute | solution.py:332
  11.3 21.1 %collective-permute-start.3 = (bf16[256,1024]{1,0:T(8,128)(2,1)}, bf16[256,1024]{1,0:T(8,128)(2,1)S(1)}, u32[]{:S(2)}, u32[]{:S(2)}) collective-permute-start(bf16[256,1024]{1,0:T(8,128)(2,1)} %collective-permute-done.2.refs_0_), channel_id=1, source_target_pairs={{0,1},{1,3},{2,0},{3,5},{4,2},{5,7},{6,4},{7,9},{8,6},{9,11},{10,8... | collective-permute-start | bytes 1572872 | tf_op jit(solution)/shard_map/ppermute | solution.py:332
  13.7 14.1 %collective-permute-start.5 = (bf16[256,1024]{1,0:T(8,128)(2,1)S(1)}, bf16[256,1024]{1,0:T(8,128)(2,1)S(1)}, u32[]{:S(2)}, u32[]{:S(2)}) collective-permute-start(bf16[256,1024]{1,0:T(8,128)(2,1)S(1)} %get-tuple-element.27.refs_0_), channel_id=1, source_target_pairs={{1,0},{3,1},{0,2},{5,3},{2,4},{7,5},{4,6},{9,7},{6,8},{11,9},{8,10... | collective-permute-start | bytes 1572872 | tf_op jit(solution)/shard_map/ppermute | solution.py:332
  16.0 14.1 %collective-permute-start.4 = (bf16[256,1024]{1,0:T(8,128)(2,1)}, bf16[256,1024]{1,0:T(8,128)(2,1)S(1)}, u32[]{:S(2)}, u32[]{:S(2)}) collective-permute-start(bf16[256,1024]{1,0:T(8,128)(2,1)} %copy-done.5), channel_id=1, source_target_pairs={{1,1},{3,0},{0,3},{5,2},{2,5},{7,4},{4,7},{9,6},{6,9},{11,8},{8,11... | collective-permute-start | bytes 1572872 | tf_op jit(solution)/shard_map/ppermute | solution.py:332
  22.7 19.2 %collective-permute-start.8 = (bf16[256,1024]{1,0:T(8,128)(2,1)S(1)}, bf16[256,1024]{1,0:T(8,128)(2,1)S(1)}, u32[]{:S(2)}, u32[]{:S(2)}) collective-permute-start(bf16[256,1024]{1,0:T(8,128)(2,1)S(1)} %collective-permute-done.6.refs_1_), channel_id=1, source_target_pairs={{1,0},{3,1},{0,2},{5,3},{2,4},{7,5},{4,6},{9,7},{6,8},{11,9},{8,10... | collective-permute-start | bytes 1572872 | tf_op jit(solution)/shard_map/ppermute | solution.py:332
  30.1 2.4 %copy-start.2 = (f32[2048]{0:T(1024)S(1)}, f32[2048]{0:T(1024)}, u32[]{:S(2)}) copy-start(f32[2048]{0:T(1024)} %param.14) | copy-start | bytes 24580
  32.5 9.5 %copy-start.1 = (bf16[128,2048]{1,0:T(8,128)(2,1)S(1)}, bf16[128,2048]{1,0:T(8,128)(2,1)}, u32[]{:S(2)}) copy-start(bf16[128,2048]{1,0:T(8,128)(2,1)} %cotangent_ref.1) | copy-start | bytes 1572868
  33.4 23.9 %collective-permute-start.7 = (bf16[128,1024]{1,0:T(8,128)(2,1)S(1)}, bf16[128,1024]{1,0:T(8,128)(2,1)S(1)}, u32[]{:S(2)}, u32[]{:S(2)}) collective-permute-start(bf16[128,1024]{1,0:T(8,128)(2,1)S(1)} %get-tuple-element.36), channel_id=1, source_target_pairs={{0,1},{1,0},{2,3},{3,2},{4,5},{5,4},{6,7},{7,6},{8,9},{9,8},{10,11... | collective-permute-start | bytes 786440 | tf_op jit(solution)/shard_map/ppermute | solution.py:332
  43.5 26.6 %all-to-all-start = ((f32[256,1,128]{2,1,0:T(1,128)}), f32[256,1,128]{2,1,0:T(1,128)S(1)}, u32[]{:S(2)}, u32[]{:S(2)}) async-start(f32[256,1,128]{2,1,0:T(1,128)} %bitcast.2), calls=%async_computation | async-start | bytes 262144 | tf_op jit(solution)/shard_map/all_to_all | solution.py:353
  57.3 0.7 copy-start.6

commit v3 on v2

--- a/solution.py
+++ b/solution.py
@@ -338,7 +338,7 @@
     kv_sib = move(kv_send, siblings)
     (qc_send,) = split_heads((1,), after(queries, kv_sib), cotangent)
     qc_sib = move(qc_send, siblings)
-    r3 = move(after(kv_own, qc_sib), backward)
+    r3 = move(after(kv_own, kv_sib), backward)
     r4 = move(after(kv_send, qc_sib), inward)
     r5 = move(r1, onward)
     bias = masks(block_keep, after(document_ids, kv_sib), link_lists)

time: 71.1 us -> 71.1 us (level)
  starting transfers between devices: 31.9 us -> 27.2 us
  waiting for transfers between devices: 17.2 us -> 21.9 us
    ppermute x9, starting transfers between devices: 18.1 us -> 13.4 us  [local(): move = lambda value, pairs: lax.ppermute(value, AXES, pairs)]
    ppermute x9, waiting for transfers between devices: 6.79 us -> 11.4 us  [local(): move = lambda value, pairs: lax.ppermute(value, AXES, pairs)]
  transfers between devices with their start and end apart: 10 -> 10, of which waited for: 6 -> 5; matrix products, arithmetic and copies ran while one was open for 0% -> 0% of each run, Pallas kernels for 26% -> 26%
where the time goes in v3:
time: 71.1 us; the launch traced here: 70.7 us
  starting transfers between devices  27.2 us (38%)
  waiting for transfers between devices  21.9 us (31%)
  Pallas kernels  20 us (28%)
  between operations  0.83 us (1%)
  local copies, waits for them, and re-layouts  0.81 us (1%)
    pallas_call x7, Pallas kernels, in_vmem(): pl.pallas_call(kernel, in_specs=[smem] * scalars + [vmem] * (len(operands...  14.4 us
    all_to_all x1, starting transfers between devices, local(): lax.all_to_all(terms.reshape(groups * shards, 1, BLK), AXES, 0, 0, tiled=...  13.8 us
    ppermute x9, starting transfers between devices, local(): move = lambda value, pairs: lax.ppermute(value, AXES, pairs)  13.4 us
    ppermute x9, waiting for transfers between devices, local(): move = lambda value, pairs: lax.ppermute(value, AXES, pairs)  11.4 us
    all_to_all x1, waiting for transfers between devices, local(): lax.all_to_all(terms.reshape(groups * shards, 1, BLK), AXES, 0, 0, tiled=...  10.4 us
    pallas_call x2, Pallas kernels, split_heads(): pl.pallas_call(functools.partial(split_kernel, sides, 2), in_specs=[pl.Bl...  2.29 us
    pallas_call x1, Pallas kernels, fill_heads(): pl.pallas_call(fill_kernel, in_specs=[pl.BlockSpec(memory_space=pltpu.VME...  1.66 us
    pallas_call x1, Pallas kernels, last_own(): pl.pallas_call(own_kernel, in_specs=[pl.BlockSpec(memory_space=pltpu.VMEM...  1.61 us
  transfers between devices with their start and end apart: 10, of which 5 were waited for; matrix products, arithmetic and copies ran while one was open for 0% of the time, Pallas kernels for 26%

profile of v3, /device:TPU:1, one launch (start us, length us, event | category | flops | bytes accessed | tf_op | source)
XLA Modules:
  0.0 70.7 jit_solution(5981696699640092632)
XLA Ops:
  0.6 1.2 %shard_map.95 = (bf16[256,1024]{1,0:T(8,128)(2,1)S(1)}, bf16[256,1024]{1,0:T(8,128)(2,1)S(1)}) custom-call(bf16[128,2048]{1,0:T(8,128)(2,1)} %refs_0_.1, bf16[128,2048]{1,0:T(8,128)(2,1)} %refs_1_.2), custom_call_target="tpu_custom_call" | custom-call | bytes 1048576 | tf_op jit(solution)/shard_map/pallas_call | solution.py:39
  1.9 3.3 %collective-permute-start = (bf16[256,1024]{1,0:T(8,128)(2,1)S(1)}, bf16[256,1024]{1,0:T(8,128)(2,1)S(1)}, u32[]{:S(2)}, u32[]{:S(2)}) collective-permute-start(bf16[256,1024]{1,0:T(8,128)(2,1)S(1)} %get-tuple-element.26), channel_id=1, source_target_pairs={{0,1},{1,0},{2,3},{3,2},{4,5},{5,4},{6,7},{7,6},{8,9},{9,8},{10,11... | collective-permute-start | bytes 1572872 | tf_op jit(solution)/shard_map/ppermute | solution.py:332
  5.2 1.5 %collective-permute-done.refs_1_ = bf16[256,1024]{1,0:T(8,128)(2,1)S(1)} collective-permute-done((bf16[256,1024]{1,0:T(8,128)(2,1)S(1)}, bf16[256,1024]{1,0:T(8,128)(2,1)S(1)}, u32[]{:S(2)}, u32[]{:S(2)}) %collective-permute-start) | collective-permute-done | bytes 524320 | tf_op jit(solution)/shard_map/ppermute | solution.py:332
  6.8 1.1 %shard_map.97 = bf16[256,1024]{1,0:T(8,128)(2,1)S(1)} custom-call(bf16[128,2048]{1,0:T(8,128)(2,1)} %query_ref.9, bf16[128,2048]{1,0:T(8,128)(2,1)} %cotangent_ref.1), custom_call_target="tpu_custom_call" | custom-call | bytes 524288 | tf_op jit(solution)/shard_map/pallas_call | solution.py:39
  7.8 0.5 collective-permute-start.1
  8.3 1.9 %collective-permute-start.6 = (bf16[256,1024]{1,0:T(8,128)(2,1)}, bf16[256,1024]{1,0:T(8,128)(2,1)S(1)}, u32[]{:S(2)}, u32[]{:S(2)}) collective-permute-start(bf16[256,1024]{1,0:T(8,128)(2,1)} %copy-done.5), channel_id=1, source_target_pairs={{0,0},{1,2},{2,1},{3,4},{4,3},{5,6},{6,5},{7,8},{8,7},{9,10},{10,9... | collective-permute-start | bytes 1572872 | tf_op jit(solution)/shard_map/ppermute | solution.py:332
  10.4 1.0 %collective-permute-done.2.refs_0_ = bf16[256,1024]{1,0:T(8,128)(2,1)} collective-permute-done((bf16[256,1024]{1,0:T(8,128)(2,1)S(1)}, bf16[256,1024]{1,0:T(8,128)(2,1)}, u32[]{:S(2)}, u32[]{:S(2)}) %collective-permute-start.2) | collective-permute-done | bytes 524320 | tf_op jit(solution)/shard_map/ppermute | solution.py:332
  11.3 2.3 %collective-permute-start.3 = (bf16[256,1024]{1,0:T(8,128)(2,1)}, bf16[256,1024]{1,0:T(8,128)(2,1)S(1)}, u32[]{:S(2)}, u32[]{:S(2)}) collective-permute-start(bf16[256,1024]{1,0:T(8,128)(2,1)} %collective-permute-done.2.refs_0_), channel_id=1, source_target_pairs={{0,1},{1,3},{2,0},{3,5},{4,2},{5,7},{6,4},{7,9},{8,6},{9,11},{10,8... | collective-permute-start | bytes 1572872 | tf_op jit(solution)/shard_map/ppermute | solution.py:332
  13.7 1.4 %shard_map.96.bias_ref = f32[1792,128]{1,0:T(8,128)S(1)} custom-call(s32[1,32,32]{2,1,0:T(8,128)S(1)} %copy-done.3, s32[1,4096]{1,0:T(1,128)S(1)} %copy-done.4, s32[1,32,8]{2,1,0:T(8,128)S(1)} %copy.12.links_ref), custom_call_target="tpu_custom_call" | custom-call | flops 67108864 | bytes 1048576 | tf_op jit(solution)/shard_map/pallas_call | solution.py:264
  15.0 1.7 %collective-permute-start.4 = (bf16[256,1024]{1,0:T(8,128)(2,1)}, bf16[256,1024]{1,0:T(8,128)(2,1)S(1)}, u32[]{:S(2)}, u32[]{:S(2)}) collective-permute-start(bf16[256,1024]{1,0:T(8,128)(2,1)} %copy-done.5), channel_id=1, source_target_pairs={{1,1},{3,0},{0,3},{5,2},{2,5},{7,4},{4,7},{9,6},{6,9},{11,8},{8,11... | collective-permute-start | bytes 1572872 | tf_op jit(solution)/shard_map/ppermute | solution.py:332
  16.7 2.8 %shard_map.98 = (f32[64,512]{1,0:T(8,128)S(1)}, f32[1024,256]{1,0:T(8,128)S(1)}) custom-call(f32[1792,128]{1,0:T(8,128)S(1)} %shard_map.96.bias_ref, bf16[128,2048]{1,0:T(8,128)(2,1)S(1)} %copy-done, bf16[256,1024]{1,0:T(8,128)(2,1)S(1)} %collective-permute-done.1.qc_sib.qc, bf16[256,1024]{1,0:T(8,128)(2,1)S(1)} %get-tuple-element.27.refs_0_, ...), custom_call_target="tpu_custom_call" | custom-call | flops 268435456 | bytes 1048576 | tf_op jit(solution)/shard_map/pallas_call | solution.py:264
  19.6 6.5 %collective-permute-done.6.refs_1_ = bf16[256,1024]{1,0:T(8,128)(2,1)S(1)} collective-permute-done((bf16[256,1024]{1,0:T(8,128)(2,1)}, bf16[256,1024]{1,0:T(8,128)(2,1)S(1)}, u32[]{:S(2)}, u32[]{:S(2)}) %collective-permute-start.6) | collective-permute-done | bytes 524320 | tf_op jit(solution)/shard_map/ppermute | solution.py:332
  26.2 4.0 %shard_map.99 = (f32[64,512]{1,0:T(8,128)S(1)}, f32[1024,256]{1,0:T(8,128)S(1)}) custom-call(f32[1792,128]{1,0:T(8,128)S(1)} %shard_map.96.bias_ref, bf16[128,2048]{1,0:T(8,128)(2,1)S(1)} %copy-done, bf16[256,1024]{1,0:T(8,128)(2,1)S(1)} %collective-permute-done.1.qc_sib.qc, bf16[256,1024]{1,0:T(8,128)(2,1)} %collective-permute-done.2.refs_0_, ...), custom_call_target="tpu_custom_call" | custom-call | flops 268435456 | bytes 1048576 | tf_op jit(solution)/shard_map/pallas_call | solution.py:264
  30.2 2.3 %shard_map.100 = (f32[64,512]{1,0:T(8,128)S(1)}, f32[1024,256]{1,0:T(8,128)S(1)}) custom-call(f32[1792,128]{1,0:T(8,128)S(1)} %shard_map.96.bias_ref, bf16[128,2048]{1,0:T(8,128)(2,1)S(1)} %copy-done, bf16[256,1024]{1,0:T(8,128)(2,1)S(1)} %collective-permute-done.1.qc_sib.qc, bf16[256,1024]{1,0:T(8,128)(2,1)S(1)} %collective-permute-done.5.refs_0_, ...), custom_call_target="tpu_custom_call" | custom-call | flops 134217728 | bytes 1048576 | tf_op jit(solution)/shard_map/pallas_call | solution.py:264
  32.6 2.3 %shard_map.101 = (f32[64,512]{1,0:T(8,128)S(1)}, f32[1024,256]{1,0:T(8,128)S(1)}) custom-call(f32[1792,128]{1,0:T(8,128)S(1)} %shard_map.96.bias_ref, bf16[128,2048]{1,0:T(8,128)(2,1)S(1)} %copy-done, bf16[256,1024]{1,0:T(8,128)(2,1)S(1)} %collective-permute-done.1.qc_sib.qc, bf16[256,1024]{1,0:T(8,128)(2,1)S(1)} %collective-permute-done.4.refs_0_, ...), custom_call_target="tpu_custom_call" | custom-call | flops 134217728 | bytes 1048576 | tf_op jit(solution)/shard_map/pallas_call | solution.py:264
  34.9 0.9 %shard_map.102 = (bf16[128,1024]{1,0:T(8,128)(2,1)S(1)}, f32[8,128]{1,0:T(8,128)S(1)}) custom-call(f32[1792,128]{1,0:T(8,128)S(1)} %shard_map.96.bias_ref, bf16[256,1024]{1,0:T(8,128)(2,1)S(1)} %collective-permute-done.1.qc_sib.qc, bf16[256,1024]{1,0:T(8,128)(2,1)S(1)} %collective-permute-done.3.kv, f32[64,512]{1,0:T(8,128)S(1)} %get-tuple-element.34.rows, ...), custom_call_target="tpu_custom_call" | custom-call | flops 67108864 | bytes 1048576 | tf_op jit(solution)/shard_map/pallas_call | solution.py:264
  35.8 3.7 %collective-permute-start.7 = (bf16[128,1024]{1,0:T(8,128)(2,1)S(1)}, bf16[128,1024]{1,0:T(8,128)(2,1)S(1)}, u32[]{:S(2)}, u32[]{:S(2)}) collective-permute-start(bf16[128,1024]{1,0:T(8,128)(2,1)S(1)} %get-tuple-element.36), channel_id=1, source_target_pairs={{0,1},{1,0},{2,3},{3,2},{4,5},{5,4},{6,7},{7,6},{8,9},{9,8},{10,11... | collective-permute-start | bytes 786440 | tf_op jit(solution)/shard_map/ppermute | solution.py:332
  39.5 2.4 %collective-permute-done.8.kv = bf16[256,1024]{1,0:T(8,128)(2,1)S(1)} collective-permute-done((bf16[256,1024]{1,0:T(8,128)(2,1)S(1)}, bf16[256,1024]{1,0:T(8,128)(2,1)S(1)}, u32[]{:S(2)}, u32[]{:S(2)}) %collective-permute-start.8) | collective-permute-done | bytes 524320 | tf_op jit(solution)/shard_map/ppermute | solution.py:332
  41.9 1.6 %shard_map.103 = (bf16[128,2048]{1,0:T(8,128)(2,1)}, f32[256,128]{1,0:T(8,128)}) custom-call(f32[1792,128]{1,0:T(8,128)S(1)} %shard_map.96.bias_ref, bf16[128,2048]{1,0:T(8,128)(2,1)S(1)} %copy-done, bf16[128,2048]{1,0:T(8,128)(2,1)S(1)} %copy-done.1, bf16[256,1024]{1,0:T(8,128)(2,1)S(1)} %collective-permute-done.8.kv, ...), custom_call_target="tpu_custom_call" | custom-call | flops 67108864 | bytes 1048576 | tf_op jit(solution)/shard_map/pallas_call | solution.py:285
  43.5 13.8 %all-to-all-start = ((f32[256,1,128]{2,1,0:T(1,128)}), f32[256,1,128]{2,1,0:T(1,128)S(1)}, u32[]{:S(2)}, u32[]{:S(2)}) async-start(f32[256,1,128]{2,1,0:T(1,128)} %bitcast.2), calls=%async_computation | async-start | bytes 262144 | tf_op jit(solution)/shard_map/all_to_all | solution.py:353
  57.3 0.7 copy-done.6
  58.0 1.7 %shard_map.104 = bf16[128,2048]{1,0:T(8,128)(2,1)} custom-call(bf16[128,1024]{1,0:T(8,128)(2,1)} %copy-done.6, bf16[128,2048]{1,0:T(8,128)(2,1)} %get-tuple-element.39.out_in), custom_call_target="tpu_custom_call", output_to_operand_aliasing={{}: (1, {})} | custom-call | bytes 1048576 | tf_op jit(solution)/shard_map/pallas_call | solution.py:244
  59.7 10.4 %all-to-all-done = f32[256,1,128]{2,1,0:T(1,128)S(1)} async-done(((f32[256,1,128]{2,1,0:T(1,128)}), f32[256,1,128]{2,1,0:T(1,128)S(1)}, u32[]{:S(2)}, u32[]{:S(2)}) %all-to-all-start) | async-done | bytes 131104 | tf_op jit(solution)/shard_map/all_to_all | solution.py:353
  70.1 0.6 shard_map.105
  (24 shorter events, 0.2 us)
Async XLA Ops:
  1.9 4.9 %copy-start.5 = (bf16[256,1024]{1,0:T(8,128)(2,1)}, bf16[256,1024]{1,0:T(8,128)(2,1)S(1)}, u32[]{:S(2)}) copy-start(bf16[256,1024]{1,0:T(8,128)(2,1)S(1)} %get-tuple-element.26) | copy-start | bytes 1572868
  1.9 4.9 %collective-permute-start = (bf16[256,1024]{1,0:T(8,128)(2,1)S(1)}, bf16[256,1024]{1,0:T(8,128)(2,1)S(1)}, u32[]{:S(2)}, u32[]{:S(2)}) collective-permute-start(bf16[256,1024]{1,0:T(8,128)(2,1)S(1)} %get-tuple-element.26), channel_id=1, source_target_pairs={{0,1},{1,0},{2,3},{3,2},{4,5},{5,4},{6,7},{7,6},{8,9},{9,8},{10,11... | collective-permute-start | bytes 1572872 | tf_op jit(solution)/shard_map/ppermute | solution.py:332
  5.2 5.0 %copy-start.7 = (s32[1,32,8]{1,2,0:T(8,128)S(1)}, s32[1,32,8]{1,2,0:T(8,128)}, u32[]{:S(2)}) copy-start(s32[1,32,8]{1,2,0:T(8,128)} %param.12) | copy-start | bytes 3076
  5.2 6.1 %collective-permute-start.2 = (bf16[256,1024]{1,0:T(8,128)(2,1)S(1)}, bf16[256,1024]{1,0:T(8,128)(2,1)}, u32[]{:S(2)}, u32[]{:S(2)}) collective-permute-start(bf16[256,1024]{1,0:T(8,128)(2,1)S(1)} %get-tuple-element.27.refs_0_), channel_id=1, source_target_pairs={{0,1},{1,3},{2,0},{3,5},{4,2},{5,7},{6,4},{7,9},{8,6},{9,11},{10,8... | collective-permute-start | bytes 1572872 | tf_op jit(solution)/shard_map/ppermute | solution.py:332
  6.8 6.9 %copy-start.3 = (s32[1,32,32]{2,1,0:T(8,128)S(1)}, s32[1,32,32]{2,1,0:T(8,128)}, u32[]{:S(2)}) copy-start(s32[1,32,32]{2,1,0:T(8,128)} %keep_ref.1) | copy-start | bytes 12292
  6.8 6.9 %copy-start.4 = (s32[1,4096]{1,0:T(1,128)S(1)}, s32[1,4096]{1,0:T(1,128)}, u32[]{:S(2)}) copy-start(s32[1,4096]{1,0:T(1,128)} %docs_ref) | copy-start | bytes 49156
  7.8 8.9 %copy-start = (bf16[128,2048]{1,0:T(8,128)(2,1)S(1)}, bf16[128,2048]{1,0:T(8,128)(2,1)}, u32[]{:S(2)}) copy-start(bf16[128,2048]{1,0:T(8,128)(2,1)} %query_ref.9) | copy-start | bytes 1572868
  7.8 7.2 %collective-permute-start.1 = (bf16[256,1024]{1,0:T(8,128)(2,1)S(1)}, bf16[256,1024]{1,0:T(8,128)(2,1)S(1)}, u32[]{:S(2)}, u32[]{:S(2)}) collective-permute-start(bf16[256,1024]{1,0:T(8,128)(2,1)S(1)} %shard_map.97), channel_id=1, source_target_pairs={{0,1},{1,0},{2,3},{3,2},{4,5},{5,4},{6,7},{7,6},{8,9},{9,8},{10,11... | collective-permute-start | bytes 1572872 | tf_op jit(solution)/shard_map/ppermute | solution.py:332
  8.3 17.9 %collective-permute-start.6 = (bf16[256,1024]{1,0:T(8,128)(2,1)}, bf16[256,1024]{1,0:T(8,128)(2,1)S(1)}, u32[]{:S(2)}, u32[]{:S(2)}) collective-permute-start(bf16[256,1024]{1,0:T(8,128)(2,1)} %copy-done.5), channel_id=1, source_target_pairs={{0,0},{1,2},{2,1},{3,4},{4,3},{5,6},{6,5},{7,8},{8,7},{9,10},{10,9... | collective-permute-start | bytes 1572872 | tf_op jit(solution)/shard_map/ppermute | solution.py:332
  10.3 19.9 %collective-permute-start.5 = (bf16[256,1024]{1,0:T(8,128)(2,1)S(1)}, bf16[256,1024]{1,0:T(8,128)(2,1)S(1)}, u32[]{:S(2)}, u32[]{:S(2)}) collective-permute-start(bf16[256,1024]{1,0:T(8,128)(2,1)S(1)} %get-tuple-element.27.refs_0_), channel_id=1, source_target_pairs={{1,0},{3,1},{0,2},{5,3},{2,4},{7,5},{4,6},{9,7},{6,8},{11,9},{8,10... | collective-permute-start | bytes 1572872 | tf_op jit(solution)/shard_map/ppermute | solution.py:332
  11.3 23.6 %collective-permute-start.3 = (bf16[256,1024]{1,0:T(8,128)(2,1)}, bf16[256,1024]{1,0:T(8,128)(2,1)S(1)}, u32[]{:S(2)}, u32[]{:S(2)}) collective-permute-start(bf16[256,1024]{1,0:T(8,128)(2,1)} %collective-permute-done.2.refs_0_), channel_id=1, source_target_pairs={{0,1},{1,3},{2,0},{3,5},{4,2},{5,7},{6,4},{7,9},{8,6},{9,11},{10,8... | collective-permute-start | bytes 1572872 | tf_op jit(solution)/shard_map/ppermute | solution.py:332
  15.0 17.5 %collective-permute-start.4 = (bf16[256,1024]{1,0:T(8,128)(2,1)}, bf16[256,1024]{1,0:T(8,128)(2,1)S(1)}, u32[]{:S(2)}, u32[]{:S(2)}) collective-permute-start(bf16[256,1024]{1,0:T(8,128)(2,1)} %copy-done.5), channel_id=1, source_target_pairs={{1,1},{3,0},{0,3},{5,2},{2,5},{7,4},{4,7},{9,6},{6,9},{11,8},{8,11... | collective-permute-start | bytes 1572872 | tf_op jit(solution)/shard_map/ppermute | solution.py:332
  26.1 15.8 %collective-permute-start.8 = (bf16[256,1024]{1,0:T(8,128)(2,1)S(1)}, bf16[256,1024]{1,0:T(8,128)(2,1)S(1)}, u32[]{:S(2)}, u32[]{:S(2)}) collective-permute-start(bf16[256,1024]{1,0:T(8,128)(2,1)S(1)} %collective-permute-done.6.refs_1_), channel_id=1, source_target_pairs={{1,0},{3,1},{0,2},{5,3},{2,4},{7,5},{4,6},{9,7},{6,8},{11,9},{8,10... | collective-permute-start | bytes 1572872 | tf_op jit(solution)/shard_map/ppermute | solution.py:332
  32.6 2.4 %copy-start.2 = (f32[2048]{0:T(1024)S(1)}, f32[2048]{0:T(1024)}, u32[]{:S(2)}) copy-start(f32[2048]{0:T(1024)} %param.14) | copy-start | bytes 24580
  34.9 7.0 %copy-start.1 = (bf16[128,2048]{1,0:T(8,128)(2,1)S(1)}, bf16[128,2048]{1,0:T(8,128)(2,1)}, u32[]{:S(2)}) copy-start(bf16[128,2048]{1,0:T(8,128)(2,1)} %cotangent_ref.1) | copy-start | bytes 1572868
  35.8 21.5 %collective-permute-start.7 = (bf16[128,1024]{1,0:T(8,128)(2,1)S(1)}, bf16[128,1024]{1,0:T(8,128)(2,1)S(1)}, u32[]{:S(2)}, u32[]{:S(2)}) collective-permute-start(bf16[128,1024]{1,0:T(8,128)(2,1)S(1)} %get-tuple-element.36), channel_id=1, source_target_pairs={{0,1},{1,0},{2,3},{3,2},{4,5},{5,4},{6,7},{7,6},{8,9},{9,8},{10,11... | collective-permute-start | bytes 786440 | tf_op jit(solution)/shard_map/ppermute | solution.py:332
  43.5 26.6 %all-to-all-start = ((f32[256,1,128]{2,1,0:T(1,128)}), f32[256,1,128]{2,1,0:T(1,128)S(1)}, u32[]{:S(2)}, u32[]{:S(2)}) async-start(f32[256,1,128]{2,1,0:T(1,128)} %bitcast.2), calls=%async_computation | async-start | bytes 262144 | tf_op jit(solution)/shard_map/all_to_all | solution.py:353
  57.3 0.7 copy-start.6
